TPU v7x, 128 devices: a whole 4x4x4 slice. The times are simulated.
128 devices in a mesh: circ: 8 (over z_lo, y), span: 16 (over z_hi, x, core).
Axes of the slice: x: 4, y: 4, z: 4 (z_hi: 2, z_lo: 2; z = z_hi * 2 + z_lo), core: 2. Of those that a mesh axis runs over, the one named last changes fastest.
Arguments:
- elem_rows: bfloat16 [80, 98304], P(None, ('circ', 'span')), may hold values from -6 to 6
- coupling: bfloat16 [48, 80, 80, 2048], P('circ', None, None, 'span')
- inverses: bfloat16 [48, 80, 80, 2048], P('circ', None, None, 'span'), may hold values from -0.625 to 0.625
- send_rows: int32 [128, 128, 12], P(('circ', 'span')), may hold values from 0 to 767, as said below
- recv_cells: int32 [128, 128, 12], P(('circ', 'span')), may hold values from 0 to 767, as said below
- slot_counts: int32 [128, 128], P(('circ', 'span')), may hold values from 0 to 12, as said below
Outputs:
- corrections: float32 [80, 98304], P(None, ('circ', 'span'))
Inputs may be any that keep to these rules, and one draw needn't show every extreme that they name: `send_rows`: each source's filled slots name each of its 768 rows exactly once, each owner's filled slots name each of its 768 cells exactly once; unfilled slots hold 0. `recv_cells`: as send_rows, for the owners' cells. `slot_counts`: every owner's counts sum to 768, and so do every source's; some pair fills all 12 slots.
All inputs are finite; a program needn't handle non-finite values.
Results may differ from a plain program's by a relative error of at most 0.0003.
Values may be sent and summed in bfloat16 or wider, within the bound.
No kernel may reach another device: no remote copies, remote signals or barrier semaphores. Data moves between devices by JAX's collectives and lax.ppermute only.
A program may use at most 128 MiB of HBM per device.

v0:
```python
import functools

import jax
import jax.numpy as jnp
from jax import lax
from jax.experimental import pallas as pl
from jax.experimental.pallas import tpu as pltpu
from jax.sharding import PartitionSpec as P

FEATURES = 80
SEGMENT = 6
LINES = 128
CELLS = SEGMENT * LINES
PEERS = 128
SLOTS = 12
PAIRS = SLOTS // 2
ROWS = 8
MAIN = 64
TAIL = FEATURES - MAIN
N_CIRC = 8

IN_VMEM = pl.BlockSpec(memory_space=pltpu.VMEM)
F32 = jnp.float32
BF16 = jnp.bfloat16


def params(megabytes):
    return pltpu.CompilerParams(vmem_limit_bytes=megabytes * 2**20)


def fold_sublanes(parts, row):
    upper = row < 4
    fours = []
    for k in range(4):
        a, b = parts[k], parts[k + 4]
        fours.append(jnp.where(upper, a, b) + pltpu.roll(jnp.where(upper, b, a), 4, 0))
    even_pair = (row & 2) == 0
    twos = []
    for k in range(2):
        a, b = fours[k], fours[k + 2]
        twos.append(jnp.where(even_pair, a + pltpu.roll(a, 6, 0), b + pltpu.roll(b, 2, 0)))
    even = (row & 1) == 0
    a, b = twos
    return jnp.where(even, a + pltpu.roll(a, 7, 0), b + pltpu.roll(b, 1, 0))


def matvec(blocks_ref, position, vector, row):
    result = []
    for group in range(FEATURES // 8):
        parts = []
        for k in range(8):
            terms = blocks_ref[position, group * 8 + k].astype(F32) * vector
            total = terms[0:8]
            for j in range(8, FEATURES, 8):
                total = total + terms[j : j + 8]
            parts.append(total)
        result.append(fold_sublanes(parts, row))
    return jnp.concatenate(result, axis=0)


def sublane_ids():
    return lax.broadcasted_iota(jnp.int32, (8, LINES), 0)


def columns(table):
    padded = jnp.concatenate([table, jnp.full((16 - SLOTS, PEERS), -1, jnp.int32)], axis=0)
    return jnp.transpose(padded)


def one_hot(index, first):
    place = lax.broadcasted_iota(jnp.int32, (PEERS, CELLS), 1)
    return jnp.concatenate(
        [
            jnp.where(index[:, 2 * pair + first : 2 * pair + first + 1] == place, 1.0, 0.0).astype(BF16)
            for pair in range(PAIRS)
        ],
        axis=0,
    )


def across(a, b):
    return lax.dot_general(a, b, (((1,), (1,)), ((), ())), preferred_element_type=F32)


def down(a, b):
    return lax.dot_general(a, b, (((0,), (0,)), ((), ())), preferred_element_type=F32)


def spread(rows, offset):
    tail_at = 128 + (0 if offset == 0 else TAIL)
    parts = [rows[:MAIN], rows[MAIN:]]
    gaps = [offset, tail_at - offset - MAIN, 256 - tail_at - TAIL]
    filled = []
    for gap, part in zip(gaps, parts + [None]):
        if gap:
            filled.append(jnp.zeros((gap, CELLS), BF16))
        if part is not None:
            filled.append(part)
    return jnp.concatenate(filled, axis=0)


def pack(pieces, index, store):
    packed = 0.0
    for first, offset in ((0, 0), (1, MAIN)):
        hot = one_hot(index, first)
        for piece in pieces:
            packed = packed + across(hot, spread(piece, offset))
    tails = []
    for pair in range(PAIRS):
        rows = packed[pair * PEERS : (pair + 1) * PEERS]
        store(pair, rows[:, :128])
        tail = rows[:, 128:]
        shift = 2 * TAIL * (pair % 4)
        tails.append(pltpu.roll(tail, shift, 1) if shift else tail)
    store(6, tails[0] + tails[1] + tails[2] + tails[3])
    store(7, tails[4] + tails[5])


def unpack(load, index, pieces):
    lane = lax.broadcasted_iota(jnp.int32, (PEERS, 128), 1)
    last = (load(6), load(7))
    total = 0.0
    for first in range(2):
        slots = []
        for pair in range(PAIRS):
            rows = load(pair)
            if first:
                rows = pltpu.roll(rows, MAIN, 1)
            shift = (MAIN - 2 * TAIL * (pair % 4) - TAIL * first) % 128
            tail = last[pair // 4]
            tail = pltpu.roll(tail, shift, 1) if shift else tail
            slots.append(jnp.where(lane < MAIN, rows, jnp.where(lane < FEATURES, tail, 0.0)))
        slots = jnp.concatenate(slots, axis=0)
        hot = one_hot(index, first)
        for _ in range(pieces):
            part = slots.astype(BF16)
            total = total + down(part, hot)
            slots = slots - part.astype(F32)
    return total[:FEATURES]


def pack_rows_kernel(rows_ref, send_ref, out_ref, wide):
    def store(r, block):
        wide[pl.ds(r, PEERS, stride=ROWS), :] = block

    pack([rows_ref[...]], columns(send_ref[...]), store)
    out_ref[...] = wide[...].astype(BF16)


def forcing_kernel(arrived_ref, cells_ref, counts_ref, inverses_ref, forcing_ref, wide, lines):
    wide[...] = arrived_ref[...].astype(F32)
    slot = lax.broadcasted_iota(jnp.int32, (SLOTS, PEERS), 0)
    cells = jnp.where(slot < counts_ref[...], cells_ref[...], -1)
    found = unpack(lambda r: wide[pl.ds(r, PEERS, stride=ROWS), :], columns(cells), 1)
    for position in range(SEGMENT):
        lines[position] = found[:, position * LINES : (position + 1) * LINES]
    row = sublane_ids()

    @pl.loop(0, SEGMENT)
    def _(position):
        forcing_ref[position] = matvec(inverses_ref, position, lines[position], row)


def hop_kernel(hop, *refs):
    if hop == 0:
        coupling_ref, forcing_ref, end_ref = refs
        state_ref = solved_ref = None
    elif hop < N_CIRC:
        state_ref, coupling_ref, forcing_ref, end_ref = refs
        solved_ref = None
    elif hop < 2 * N_CIRC - 1:
        state_ref, coupling_ref, forcing_ref, end_ref, solved_ref = refs
    else:
        state_ref, coupling_ref, forcing_ref, solved_ref = refs
        end_ref = None

    @pl.when(lax.axis_index("circ") == hop % N_CIRC)
    def _():
        row = sublane_ids()

        def step(position, state):
            state = forcing_ref[position] + matvec(coupling_ref, position, state, row)
            if solved_ref is not None:
                solved_ref[position] = state
            return state

        if hop == 0:
            state = lax.fori_loop(1, SEGMENT, step, forcing_ref[0])
        else:
            state = lax.fori_loop(0, SEGMENT, step, state_ref[...])
        if end_ref is not None:
            end_ref[...] = state


def return_pack_kernel(solved_ref, cells_ref, counts_ref, out_ref):
    def store(r, block):
        out_ref[pl.ds(r, PEERS, stride=ROWS), :] = block

    slot = lax.broadcasted_iota(jnp.int32, (SLOTS, PEERS), 0)
    cells = jnp.where(slot < counts_ref[...], cells_ref[...], -1)
    rest = jnp.concatenate([solved_ref[position] for position in range(SEGMENT)], axis=1)
    high = rest.astype(BF16)
    low = (rest - high.astype(F32)).astype(BF16)
    pack([high, low], columns(cells), store)


def return_kernel(arrived_ref, send_ref, out_ref):
    out_ref[...] = unpack(
        lambda r: arrived_ref[pl.ds(r, PEERS, stride=ROWS), :], columns(send_ref[...]), 2
    )


def vmem(x):
    return pltpu.with_memory_space_constraint(x, pltpu.VMEM)


def exchange(rows):
    blocks = rows.reshape(PEERS, ROWS, 128)
    moved = lax.all_to_all(blocks, ("circ", "span"), split_axis=0, concat_axis=0, tiled=True)
    return moved.reshape(PEERS * ROWS, 128)


def local(elem_rows, coupling, inverses, send_rows, recv_cells, slot_counts):
    send = jnp.transpose(send_rows[0])
    cells = jnp.transpose(recv_cells[0])
    packed_rows = (PEERS * ROWS, 128)
    state_shape = jax.ShapeDtypeStruct((FEATURES, LINES), F32)
    forcing_shape = jax.ShapeDtypeStruct((SEGMENT, FEATURES, LINES), F32)
    outgoing = pl.pallas_call(
        pack_rows_kernel,
        out_shape=jax.ShapeDtypeStruct(packed_rows, BF16),
        in_specs=[IN_VMEM] * 2,
        out_specs=IN_VMEM,
        scratch_shapes=[pltpu.VMEM(packed_rows, F32)],
        compiler_params=params(16),
        name="pack_rows",
    )(elem_rows, send)
    arrived = exchange(outgoing)
    coupling = vmem(coupling)
    forcing = pl.pallas_call(
        forcing_kernel,
        out_shape=forcing_shape,
        in_specs=[IN_VMEM] * 4,
        out_specs=IN_VMEM,
        scratch_shapes=[
            pltpu.VMEM(packed_rows, F32),
            pltpu.VMEM((SEGMENT, FEATURES, LINES), F32),
        ],
        compiler_params=params(16),
        name="forcing",
    )(arrived, cells, slot_counts, vmem(inverses))

    state = None
    for hop in range(2 * N_CIRC):
        operands = ([] if hop == 0 else [state]) + [coupling, vmem(forcing)]
        second, final = hop >= N_CIRC, hop == 2 * N_CIRC - 1
        shapes = ([] if final else [state_shape]) + ([forcing_shape] if second else [])
        results = pl.pallas_call(
            functools.partial(hop_kernel, hop),
            out_shape=shapes,
            in_specs=[IN_VMEM] * len(operands),
            out_specs=[IN_VMEM] * len(shapes),
            input_output_aliases={len(operands) - 1: len(shapes) - 1} if second else {},
            compiler_params=params(8),
            name="hop",
        )(*operands)
        if second:
            forcing = results[-1]
        if not final:
            here = hop % N_CIRC
            state = lax.ppermute(results[0], "circ", [(here, (here + 1) % N_CIRC)])

    returning = pl.pallas_call(
        return_pack_kernel,
        out_shape=jax.ShapeDtypeStruct(packed_rows, F32),
        in_specs=[IN_VMEM] * 3,
        out_specs=IN_VMEM,
        compiler_params=params(16),
        name="return_pack",
    )(forcing, cells, slot_counts)
    returned = exchange(returning)
    return pl.pallas_call(
        return_kernel,
        out_shape=jax.ShapeDtypeStruct((FEATURES, CELLS), F32),
        in_specs=[IN_VMEM] * 2,
        out_specs=IN_VMEM,
        compiler_params=params(16),
        name="return_rows",
    )(returned, send)


def solution(mesh):
    return jax.shard_map(
        local,
        mesh=mesh,
        in_specs=(
            P(None, ("circ", "span")),
            P("circ", None, None, "span"),
            P("circ", None, None, "span"),
            P(("circ", "span"), None, None),
            P(("circ", "span"), None, None),
            P(("circ", "span"), None),
        ),
        out_specs=P(None, ("circ", "span")),
        check_vma=False,
    )
```

profile of v0, /device:TPU:1, one launch (start us, length us, event | category | flops | bytes accessed | tf_op | source)
XLA Modules:
  0.0 157.4 jit_solution(2821649332061744723)
XLA Ops:
  0.0 0.7 copy.20
  0.7 0.0 copy-start.2
  0.7 0.9 copy-done.2
  1.6 1.8 %pack_rows.1 = bf16[1024,128]{1,0:T(8,128)(2,1)} custom-call(bf16[80,768]{1,0:T(8,128)(2,1)S(1)} %copy-done.2, s32[12,128]{1,0:T(8,128)S(1)} %bitcast.19), custom_call_target="tpu_custom_call" | custom-call | tf_op jit(solution)/shard_map/pack_rows/pallas_call | solution.py:229
  3.4 11.5 %all-to-all-start = ((bf16[128,8,128]{2,1,0:T(8,128)(2,1)}), bf16[128,8,128]{2,1,0:T(8,128)(2,1)S(1)}, u32[]{:S(2)}, u32[]{:S(2)}) async-start(bf16[128,8,128]{2,1,0:T(8,128)(2,1)} %bitcast.1), calls=%async_computation | async-start | bytes 524288 | tf_op jit(solution)/shard_map/all_to_all | solution.py:219
  14.9 0.7 copy.19
  15.6 10.2 %all-to-all-done = bf16[128,8,128]{2,1,0:T(8,128)(2,1)S(1)} async-done(((bf16[128,8,128]{2,1,0:T(8,128)(2,1)}), bf16[128,8,128]{2,1,0:T(8,128)(2,1)S(1)}, u32[]{:S(2)}, u32[]{:S(2)}) %all-to-all-start) | async-done | bytes 262176 | tf_op jit(solution)/shard_map/all_to_all | solution.py:219
  25.8 0.0 copy-start
  25.8 0.0 copy-start.1
  25.8 3.9 %copy-done.1 = bf16[6,80,80,128]{3,2,1,0:T(8,128)(2,1)S(1)} copy-done((bf16[6,80,80,128]{3,2,1,0:T(8,128)(2,1)S(1)}, bf16[6,80,80,128]{3,2,1,0:T(8,128)(2,1)}, u32[]{:S(2)}) %copy-start.1) | copy-done | bytes 9830424
  29.7 0.9 copy-done.3
  30.6 3.4 %forcing.1.refs_1_.refs_2_ = f32[6,80,128]{2,1,0:T(8,128)S(1)} custom-call(bf16[1024,128]{1,0:T(8,128)(2,1)S(1)} %bitcast.16, s32[12,128]{1,0:T(8,128)S(1)} %bitcast.17, s32[1,128]{1,0:T(1,128)S(1)} %copy-done.3, bf16[6,80,80,128]{3,2,1,0:T(8,128)(2,1)S(1)} %copy-done.1), custom_call_target="tpu_custom_call" | custom-call | tf_op jit(solution)/shard_map/forcing/pallas_call | solution.py:240
  34.0 0.0 copy-done
  34.1 1.8 %hop.16 = f32[80,128]{1,0:T(8,128)S(1)} custom-call(bf16[6,80,80,128]{3,2,1,0:T(8,128)(2,1)S(1)} %copy-done, f32[6,80,128]{2,1,0:T(8,128)S(1)} %forcing.1.refs_1_.refs_2_), custom_call_target="tpu_custom_call" | custom-call | tf_op jit(solution)/shard_map/hop/pallas_call | solution.py:258
  35.9 1.3 collective-permute-start
  37.2 1.1 collective-permute-done.refs_0_
  38.2 0.7 collective-permute-start.1
  38.9 0.0 collective-permute-done.1.refs_0_
  38.9 0.7 collective-permute-start.2
  39.6 0.0 collective-permute-done.2.refs_0_
  39.7 0.7 collective-permute-start.3
  40.3 0.0 collective-permute-done.3.refs_0_
  40.4 0.7 collective-permute-start.4
  41.0 0.0 collective-permute-done.4.refs_0_
  41.1 0.7 collective-permute-start.5
  41.7 0.0 collective-permute-done.5.refs_0_
  41.8 0.7 collective-permute-start.6
  42.4 0.0 collective-permute-done.6.refs_0_
  42.5 1.3 collective-permute-start.7
  43.8 36.5 %collective-permute-done.7.refs_0_ = f32[80,128]{1,0:T(8,128)S(1)} collective-permute-done((f32[80,128]{1,0:T(8,128)S(1)}, f32[80,128]{1,0:T(8,128)S(1)}, u32[]{:S(2)}, u32[]{:S(2)}) %collective-permute-start.7) | collective-permute-done | bytes 40992 | tf_op jit(solution)/shard_map/ppermute | solution.py:271
  80.3 2.2 %hop.24 = (f32[80,128]{1,0:T(8,128)S(1)}, f32[6,80,128]{2,1,0:T(8,128)S(1)}) custom-call(f32[80,128]{1,0:T(8,128)S(1)} %collective-permute-done.7.refs_0_, bf16[6,80,80,128]{3,2,1,0:T(8,128)(2,1)S(1)} %copy-done, f32[6,80,128]{2,1,0:T(8,128)S(1)} %forcing.1.refs_1_.refs_2_), custom_call_target="tpu_custom_call", output_to_operand_aliasing={{1}: (2, {})} | custom-call | tf_op jit(solution)/shard_map/hop/pallas_call | solution.py:258
  82.5 1.3 collective-permute-start.8
  83.8 1.1 collective-permute-done.8.refs_0_
  84.8 0.7 collective-permute-start.9
  85.5 0.0 collective-permute-done.9.refs_0_
  85.5 0.7 collective-permute-start.10
  86.2 0.0 collective-permute-done.10.refs_0_
  86.2 0.7 collective-permute-start.11
  86.9 0.0 collective-permute-done.11.refs_0_
  86.9 0.7 collective-permute-start.12
  87.6 0.0 collective-permute-done.12.refs_0_
  87.7 0.7 collective-permute-start.13
  88.3 0.0 collective-permute-done.13.refs_0_
  88.4 0.7 collective-permute-start.14
  89.0 0.0 collective-permute-done.14.refs_0_
  89.1 1.6 %return_pack.1 = f32[1024,128]{1,0:T(8,128)S(1)} custom-call(f32[6,80,128]{2,1,0:T(8,128)S(1)} %hop.31.solved_ref, s32[12,128]{1,0:T(8,128)S(1)} %bitcast.18, s32[1,128]{1,0:T(1,128)S(1)} %copy-done.3), custom_call_target="tpu_custom_call" | custom-call | tf_op jit(solution)/shard_map/return_pack/pallas_call | solution.py:273
  90.7 64.4 %all_to_all.10 = f32[128,8,128]{2,1,0:T(8,128)S(1)} all-to-all(f32[128,8,128]{2,1,0:T(8,128)S(1)} %bitcast.14), channel_id=1, replica_groups=mesh['circ'=8,'span'=16] {'circ','span'}, dimensions={0} | all-to-all | bytes 1048576 | tf_op jit(solution)/shard_map/all_to_all | solution.py:219
  155.1 2.3 %return_rows.1 = f32[80,768]{1,0:T(8,128)} custom-call(f32[1024,128]{1,0:T(8,128)S(1)} %bitcast.15, s32[12,128]{1,0:T(8,128)S(1)} %bitcast.20), custom_call_target="tpu_custom_call" | custom-call | tf_op jit(solution)/shard_map/return_rows/pallas_call | solution.py:282
  (15 shorter events, 0.2 us)
Async XLA Ops:
  0.7 0.9 copy-start.2
  3.4 22.4 %all-to-all-start = ((bf16[128,8,128]{2,1,0:T(8,128)(2,1)}), bf16[128,8,128]{2,1,0:T(8,128)(2,1)S(1)}, u32[]{:S(2)}, u32[]{:S(2)}) async-start(bf16[128,8,128]{2,1,0:T(8,128)(2,1)} %bitcast.1), calls=%async_computation | async-start | bytes 524288 | tf_op jit(solution)/shard_map/all_to_all | solution.py:219
  25.8 8.3 %copy-start = (bf16[6,80,80,128]{3,2,1,0:T(8,128)(2,1)S(1)}, bf16[6,80,80,128]{3,2,1,0:T(8,128)(2,1)}, u32[]{:S(2)}) copy-start(bf16[6,80,80,128]{3,2,1,0:T(8,128)(2,1)} %refs_1_.29) | copy-start | bytes 29491204
  25.8 3.9 %copy-start.1 = (bf16[6,80,80,128]{3,2,1,0:T(8,128)(2,1)S(1)}, bf16[6,80,80,128]{3,2,1,0:T(8,128)(2,1)}, u32[]{:S(2)}) copy-start(bf16[6,80,80,128]{3,2,1,0:T(8,128)(2,1)} %inverses_ref.1) | copy-start | bytes 29491204
  29.7 0.9 copy-start.3
  35.9 2.4 %collective-permute-start = (f32[80,128]{1,0:T(8,128)S(1)}, f32[80,128]{1,0:T(8,128)S(1)}, u32[]{:S(2)}, u32[]{:S(2)}) collective-permute-start(f32[80,128]{1,0:T(8,128)S(1)} %hop.16), channel_id=1, source_target_pairs={{0,16},{1,17},{2,18},{3,19},{4,20},{5,21},{6,22},{7,23},{8,24},{9,... | collective-permute-start | bytes 122888 | tf_op jit(solution)/shard_map/ppermute | solution.py:271
  38.2 0.7 collective-permute-start.1
  38.9 0.7 collective-permute-start.2
  39.7 0.7 collective-permute-start.3
  40.4 0.7 collective-permute-start.4
  41.1 0.7 collective-permute-start.5
  41.8 0.7 collective-permute-start.6
  42.5 37.8 %collective-permute-start.7 = (f32[80,128]{1,0:T(8,128)S(1)}, f32[80,128]{1,0:T(8,128)S(1)}, u32[]{:S(2)}, u32[]{:S(2)}) collective-permute-start(f32[80,128]{1,0:T(8,128)S(1)} %hop.23), channel_id=1, source_target_pairs={{112,0},{113,1},{114,2},{115,3},{116,4},{117,5},{118,6},{119,7},{1... | collective-permute-start | bytes 122888 | tf_op jit(solution)/shard_map/ppermute | solution.py:271
  82.5 2.4 %collective-permute-start.8 = (f32[80,128]{1,0:T(8,128)S(1)}, f32[80,128]{1,0:T(8,128)S(1)}, u32[]{:S(2)}, u32[]{:S(2)}) collective-permute-start(f32[80,128]{1,0:T(8,128)S(1)} %get-tuple-element.19), channel_id=1, source_target_pairs={{0,16},{1,17},{2,18},{3,19},{4,20},{5,21},{6,22},{7,23},{8,24},{9,... | collective-permute-start | bytes 122888 | tf_op jit(solution)/shard_map/ppermute | solution.py:271
  84.8 0.7 collective-permute-start.9
  85.5 0.7 collective-permute-start.10
  86.2 0.7 collective-permute-start.11
  86.9 0.7 collective-permute-start.12
  87.7 0.7 collective-permute-start.13
  88.4 0.7 collective-permute-start.14
where the time goes:
time: 158 us; the launch traced here: 157 us
  blocking collectives  64.4 us (41%)
  waiting for transfers between devices  48.9 us (31%)
  starting transfers between devices  23.3 us (15%)
  Pallas kernels  13.3 us (8%)
  local copies, waits for them, and re-layouts  7.15 us (5%)
    all_to_all x1, blocking collectives, exchange(): lax.all_to_all(blocks, ('circ', 'span'), split_axis=0, concat_axis=0, til...  64.4 us
    ppermute x15, waiting for transfers between devices, local(): state = lax.ppermute(results[0], 'circ', [(here, (here + 1) % N_CIRC)])  38.7 us
    ppermute x15, starting transfers between devices, local(): state = lax.ppermute(results[0], 'circ', [(here, (here + 1) % N_CIRC)])  11.8 us
    all_to_all x1, starting transfers between devices, exchange(): lax.all_to_all(blocks, ('circ', 'span'), split_axis=0, concat_axis=0, til...  11.5 us
    all_to_all x1, waiting for transfers between devices, exchange(): lax.all_to_all(blocks, ('circ', 'span'), split_axis=0, concat_axis=0, til...  10.2 us
    unnamed x10, local copies, waits for them, and re-layouts  7.15 us
    pallas_call x16, Pallas kernels, local(): pl.pallas_call(functools.partial(hop_kernel, hop), out_shape=shapes, in_s...  4.17 us
    pallas_call x1, Pallas kernels, local(): pl.pallas_call(forcing_kernel, out_shape=forcing_shape, in_specs=[IN_VMEM...  3.41 us
  transfers between devices with their start and end apart: 16, of which 4 were waited for; matrix products, arithmetic and copies ran while one was open for 0% of the time, Pallas kernels for 0%

commit v1 on v0

--- a/solution.py
+++ b/solution.py
@@ -18,6 +18,9 @@
 MAIN = 64
 TAIL = FEATURES - MAIN
 N_CIRC = 8
+HALF = FEATURES // 2
+LANES = 128
+SIDE = LANES // 2
 
 IN_VMEM = pl.BlockSpec(memory_space=pltpu.VMEM)
 F32 = jnp.float32
@@ -46,7 +49,7 @@
 
 def matvec(blocks_ref, position, vector, row):
     result = []
-    for group in range(FEATURES // 8):
+    for group in range(blocks_ref.shape[1] // 8):
         parts = []
         for k in range(8):
             terms = blocks_ref[position, group * 8 + k].astype(F32) * vector
@@ -99,10 +102,17 @@
     return jnp.concatenate(filled, axis=0)
 
 
-def pack(pieces, index, store):
+def swap(x):
+    return pltpu.roll(x, SIDE, 1)
+
+
+def left(rows):
+    return lax.broadcasted_iota(jnp.int32, (rows, LANES), 1) < SIDE
+
+
+def pack(pieces, hots, store):
     packed = 0.0
-    for first, offset in ((0, 0), (1, MAIN)):
-        hot = one_hot(index, first)
+    for hot, offset in zip(hots, (0, MAIN)):
         for piece in pieces:
             packed = packed + across(hot, spread(piece, offset))
     tails = []
@@ -116,7 +126,7 @@
     store(7, tails[4] + tails[5])
 
 
-def unpack(load, index, pieces):
+def unpack(load, hots, pieces):
     lane = lax.broadcasted_iota(jnp.int32, (PEERS, 128), 1)
     last = (load(6), load(7))
     total = 0.0
@@ -131,7 +141,7 @@
             tail = pltpu.roll(tail, shift, 1) if shift else tail
             slots.append(jnp.where(lane < MAIN, rows, jnp.where(lane < FEATURES, tail, 0.0)))
         slots = jnp.concatenate(slots, axis=0)
-        hot = one_hot(index, first)
+        hot = hots[first]
         for _ in range(pieces):
             part = slots.astype(BF16)
             total = total + down(part, hot)
@@ -143,75 +153,135 @@
     def store(r, block):
         wide[pl.ds(r, PEERS, stride=ROWS), :] = block
 
-    pack([rows_ref[...]], columns(send_ref[...]), store)
+    index = columns(send_ref[...])
+    pack([rows_ref[...]], (one_hot(index, 0), one_hot(index, 1)), store)
     out_ref[...] = wide[...].astype(BF16)
 
 
-def forcing_kernel(arrived_ref, cells_ref, counts_ref, inverses_ref, forcing_ref, wide, lines):
+def bundle_kernel(coupling_ref, bundle_a, bundle_b):
+    on_left = left(HALF)
+
+    @pl.loop(0, coupling_ref.shape[2])
+    def _(i):
+        low = coupling_ref[0, 0, i].astype(F32)
+        high = coupling_ref[0, 1, i].astype(F32)
+        for ref, a, b in ((bundle_a, low, swap(high)), (bundle_b, swap(low), high)):
+            same = jnp.where(on_left, a[:HALF], b[HALF:])
+            cross = jnp.where(on_left, a[HALF:], b[:HALF])
+            ref[0, i] = jnp.concatenate([same, cross], axis=0).astype(BF16)
+
+
+def forcing_kernel(
+    arrived_ref, cells_ref, counts_ref, inverses_hbm, bundle_hbm,
+    forcing_a, forcing_b, even_ref, odd_ref, bundle_ref,
+    wide, lines, inverses_ref, sems, bundle_sem,
+):
+    copies = [
+        pltpu.make_async_copy(inverses_hbm.at[p], inverses_ref.at[p], sems.at[p])
+        for p in range(SEGMENT)
+    ]
+    for copy in copies:
+        copy.start()
+    bundle_copy = pltpu.make_async_copy(bundle_hbm, bundle_ref, bundle_sem)
+    bundle_copy.start()
     wide[...] = arrived_ref[...].astype(F32)
     slot = lax.broadcasted_iota(jnp.int32, (SLOTS, PEERS), 0)
-    cells = jnp.where(slot < counts_ref[...], cells_ref[...], -1)
-    found = unpack(lambda r: wide[pl.ds(r, PEERS, stride=ROWS), :], columns(cells), 1)
-    for position in range(SEGMENT):
-        lines[position] = found[:, position * LINES : (position + 1) * LINES]
+    index = columns(jnp.where(slot < counts_ref[...], cells_ref[...], -1))
+    hots = one_hot(index, 0), one_hot(index, 1)
+    even_ref[...], odd_ref[...] = hots
+    found = unpack(lambda r: wide[pl.ds(r, PEERS, stride=ROWS), :], hots, 1)
+    for p in range(SEGMENT):
+        lines[p] = found[:, p * LINES : (p + 1) * LINES]
     row = sublane_ids()
-
-    @pl.loop(0, SEGMENT)
-    def _(position):
-        forcing_ref[position] = matvec(inverses_ref, position, lines[position], row)
+    on_left = left(HALF)
+    for p in range(SEGMENT):
+        copies[p].wait()
+        forcing = matvec(inverses_ref, p, lines[p], row)
+        low, high = forcing[:HALF], forcing[HALF:]
+        forcing_a[p] = jnp.where(on_left, low, swap(high))
+        forcing_b[p] = jnp.where(on_left, swap(low), high)
+    bundle_copy.wait()
+
+
+def advance(coupling_ref, forcing_ref, first, state, record=None):
+    row = sublane_ids()
+
+    def step(position, state):
+        both = jnp.concatenate([state, swap(state)], axis=0)
+        state = forcing_ref[position] + matvec(coupling_ref, position, both, row)
+        if record is not None:
+            record[position] = state
+        return state
+
+    return lax.fori_loop(first, SEGMENT, step, state)
+
+
+def here(hop):
+    return lax.axis_index("circ") == hop % N_CIRC
+
+
+def first_hop_kernel(bundle_hbm, coupling_ref, forcing_ref, end_ref, bundle_ref, sem):
+    copy = pltpu.make_async_copy(bundle_hbm, bundle_ref, sem)
+    copy.start()
+
+    @pl.when(here(0))
+    def _():
+        end_ref[...] = advance(coupling_ref, forcing_ref, 1, forcing_ref[0])
+
+    copy.wait()
 
 
 def hop_kernel(hop, *refs):
-    if hop == 0:
-        coupling_ref, forcing_ref, end_ref = refs
-        state_ref = solved_ref = None
-    elif hop < N_CIRC:
-        state_ref, coupling_ref, forcing_ref, end_ref = refs
-        solved_ref = None
-    elif hop < 2 * N_CIRC - 1:
-        state_ref, coupling_ref, forcing_ref, end_ref, solved_ref = refs
-    else:
-        state_ref, coupling_ref, forcing_ref, solved_ref = refs
-        end_ref = None
-
-    @pl.when(lax.axis_index("circ") == hop % N_CIRC)
+    *state_refs, coupling_ref, forcing_ref, end_ref = refs
+
+    @pl.when(here(hop))
     def _():
-        row = sublane_ids()
-
-        def step(position, state):
-            state = forcing_ref[position] + matvec(coupling_ref, position, state, row)
-            if solved_ref is not None:
-                solved_ref[position] = state
-            return state
-
-        if hop == 0:
-            state = lax.fori_loop(1, SEGMENT, step, forcing_ref[0])
+        if state_refs:
+            end_ref[...] = advance(coupling_ref, forcing_ref, 0, state_refs[0][...])
         else:
-            state = lax.fori_loop(0, SEGMENT, step, state_ref[...])
-        if end_ref is not None:
-            end_ref[...] = state
-
-
-def return_pack_kernel(solved_ref, cells_ref, counts_ref, out_ref):
+            end_ref[...] = advance(coupling_ref, forcing_ref, 1, forcing_ref[0])
+
+
+def final_kernel(*refs):
+    *state_refs, coupling_ref, forcing_ref, solved_ref = refs
+    state = state_refs[0][...]
+    for ref in state_refs[1:]:
+        state = state + ref[...]
+    advance(coupling_ref, forcing_ref, 0, state, solved_ref)
+
+
+def return_pack_kernel(solved_a, solved_b, even_ref, odd_ref, out_ref):
     def store(r, block):
         out_ref[pl.ds(r, PEERS, stride=ROWS), :] = block
 
-    slot = lax.broadcasted_iota(jnp.int32, (SLOTS, PEERS), 0)
-    cells = jnp.where(slot < counts_ref[...], cells_ref[...], -1)
-    rest = jnp.concatenate([solved_ref[position] for position in range(SEGMENT)], axis=1)
+    on_left = left(HALF)
+    cells = []
+    for position in range(SEGMENT):
+        a, b = solved_a[position], solved_b[position]
+        low = jnp.where(on_left, a, swap(b))
+        high = jnp.where(on_left, swap(a), b)
+        cells.append(jnp.concatenate([low, high], axis=0))
+    rest = jnp.concatenate(cells, axis=1)
     high = rest.astype(BF16)
     low = (rest - high.astype(F32)).astype(BF16)
-    pack([high, low], columns(cells), store)
+    pack([high, low], (even_ref[...], odd_ref[...]), store)
 
 
 def return_kernel(arrived_ref, send_ref, out_ref):
+    index = columns(send_ref[...])
     out_ref[...] = unpack(
-        lambda r: arrived_ref[pl.ds(r, PEERS, stride=ROWS), :], columns(send_ref[...]), 2
+        lambda r: arrived_ref[pl.ds(r, PEERS, stride=ROWS), :],
+        (one_hot(index, 0), one_hot(index, 1)),
+        2,
     )
 
 
 def vmem(x):
     return pltpu.with_memory_space_constraint(x, pltpu.VMEM)
+
+
+def hbm(x):
+    return pltpu.with_memory_space_constraint(x, pltpu.HBM)
 
 
 def exchange(rows):
@@ -223,9 +293,12 @@
 def local(elem_rows, coupling, inverses, send_rows, recv_cells, slot_counts):
     send = jnp.transpose(send_rows[0])
     cells = jnp.transpose(recv_cells[0])
-    packed_rows = (PEERS * ROWS, 128)
-    state_shape = jax.ShapeDtypeStruct((FEATURES, LINES), F32)
-    forcing_shape = jax.ShapeDtypeStruct((SEGMENT, FEATURES, LINES), F32)
+    packed_rows = (PEERS * ROWS, LANES)
+    hot_shape = jax.ShapeDtypeStruct((PAIRS * PEERS, CELLS), BF16)
+    bundle_shape = jax.ShapeDtypeStruct((SEGMENT, HALF, FEATURES, LANES), BF16)
+    state_shape = jax.ShapeDtypeStruct((HALF, LANES), F32)
+    forcing_shape = jax.ShapeDtypeStruct((SEGMENT, HALF, LANES), F32)
+    in_hbm = pl.BlockSpec(memory_space=pltpu.HBM)
     outgoing = pl.pallas_call(
         pack_rows_kernel,
         out_shape=jax.ShapeDtypeStruct(packed_rows, BF16),
@@ -236,48 +309,86 @@
         name="pack_rows",
     )(elem_rows, send)
     arrived = exchange(outgoing)
-    coupling = vmem(coupling)
-    forcing = pl.pallas_call(
+    split = 2
+    bundles = pl.pallas_call(
+        bundle_kernel,
+        out_shape=[bundle_shape] * 2,
+        grid=(SEGMENT, split),
+        in_specs=[
+            pl.BlockSpec((1, 2, HALF // split, FEATURES, LANES), lambda p, k: (p, 0, k, 0, 0))
+        ],
+        out_specs=[pl.BlockSpec((1, HALF // split, FEATURES, LANES), lambda p, k: (p, k, 0, 0))] * 2,
+        compiler_params=params(16),
+        cost_estimate=pl.CostEstimate(flops=0, bytes_accessed=4 * coupling.size, transcendentals=0),
+        name="bundle",
+    )(hbm(coupling.reshape(SEGMENT, 2, HALF, FEATURES, LANES)))
+    *forcings, even, odd, bundle_a = pl.pallas_call(
         forcing_kernel,
-        out_shape=forcing_shape,
-        in_specs=[IN_VMEM] * 4,
-        out_specs=IN_VMEM,
+        out_shape=[forcing_shape] * 2 + [hot_shape] * 2 + [bundle_shape],
+        in_specs=[IN_VMEM] * 3 + [in_hbm] * 2,
+        out_specs=[IN_VMEM] * 5,
         scratch_shapes=[
             pltpu.VMEM(packed_rows, F32),
             pltpu.VMEM((SEGMENT, FEATURES, LINES), F32),
+            pltpu.VMEM(inverses.shape, BF16),
+            pltpu.SemaphoreType.DMA((SEGMENT,)),
+            pltpu.SemaphoreType.DMA,
         ],
-        compiler_params=params(16),
+        compiler_params=params(24),
         name="forcing",
-    )(arrived, cells, slot_counts, vmem(inverses))
-
-    state = None
-    for hop in range(2 * N_CIRC):
-        operands = ([] if hop == 0 else [state]) + [coupling, vmem(forcing)]
-        second, final = hop >= N_CIRC, hop == 2 * N_CIRC - 1
-        shapes = ([] if final else [state_shape]) + ([forcing_shape] if second else [])
-        results = pl.pallas_call(
-            functools.partial(hop_kernel, hop),
-            out_shape=shapes,
+    )(arrived, cells, slot_counts, hbm(inverses), hbm(bundles[0]))
+    even, odd = vmem(even), vmem(odd)
+    bundle_a = vmem(bundle_a)
+    forcings = [vmem(forcing) for forcing in forcings]
+    end_a, bundle_b = pl.pallas_call(
+        first_hop_kernel,
+        out_shape=[state_shape, bundle_shape],
+        in_specs=[in_hbm] + [IN_VMEM] * 2,
+        out_specs=[IN_VMEM] * 2,
+        scratch_shapes=[pltpu.SemaphoreType.DMA],
+        compiler_params=params(8),
+        name="hop_a",
+    )(hbm(bundles[1]), bundle_a, forcings[0])
+    bundles = [bundle_a, vmem(bundle_b)]
+
+    def sweep(side, kernel, states, shape, name):
+        operands = [*states, bundles[side], forcings[side]]
+        return pl.pallas_call(
+            kernel,
+            out_shape=shape,
             in_specs=[IN_VMEM] * len(operands),
-            out_specs=[IN_VMEM] * len(shapes),
-            input_output_aliases={len(operands) - 1: len(shapes) - 1} if second else {},
+            out_specs=IN_VMEM,
             compiler_params=params(8),
-            name="hop",
+            cost_estimate=pl.CostEstimate(
+                flops=2 * 10**6, bytes_accessed=2 * bundle_shape.size, transcendentals=0
+            ),
+            name=name + "ab"[side],
         )(*operands)
-        if second:
-            forcing = results[-1]
-        if not final:
-            here = hop % N_CIRC
-            state = lax.ppermute(results[0], "circ", [(here, (here + 1) % N_CIRC)])
+
+    arrivals = ([], [])
+    for hop in range(2 * N_CIRC - 1):
+        for side in range(2):
+            if hop == 0 and side == 0:
+                end = end_a
+            else:
+                end = sweep(
+                    side, functools.partial(hop_kernel, hop), arrivals[side][-1:], state_shape, "hop_"
+                )
+            pair = (hop % N_CIRC, (hop + 1) % N_CIRC)
+            arrivals[side].append(lax.ppermute(end, "circ", [pair]))
+    solved = [
+        sweep(side, final_kernel, arrivals[side][N_CIRC - 1 :], forcing_shape, "final_")
+        for side in range(2)
+    ]
 
     returning = pl.pallas_call(
         return_pack_kernel,
         out_shape=jax.ShapeDtypeStruct(packed_rows, F32),
-        in_specs=[IN_VMEM] * 3,
+        in_specs=[IN_VMEM] * 4,
         out_specs=IN_VMEM,
         compiler_params=params(16),
         name="return_pack",
-    )(forcing, cells, slot_counts)
+    )(*solved, even, odd)
     returned = exchange(returning)
     return pl.pallas_call(
         return_kernel,

time: 158 us -> 164 us (1.038)
  Pallas kernels: 13.3 us -> 42.4 us
  waiting for transfers between devices: 48.9 us -> 23.3 us
  starting transfers between devices: 23.3 us -> 36.1 us
  blocking collectives: 64.4 us -> 53.6 us
    pallas_call x17 -> x34, Pallas kernels: 7.58 us -> 36.5 us  [the longest x1 21.1 us: local(): pl.pallas_call(bundle_kernel, out_shape=[bundle_shape] * 2, grid=(SEGMENT...]
    ppermute x15 -> x30, waiting for transfers between devices: 38.7 us -> 23.3 us  [local(): arrivals[side].append(lax.ppermute(end, 'circ', [pair]))]
    ppermute x15 -> x30, starting transfers between devices: 11.8 us -> 24.6 us  [local(): arrivals[side].append(lax.ppermute(end, 'circ', [pair]))]
    all_to_all x1, blocking collectives: 64.4 us -> 53.6 us  [exchange(): lax.all_to_all(blocks, ('circ', 'span'), split_axis=0, concat_axis=0, til...]
    all_to_all x1, waiting for transfers between devices: 10.2 us -> 0.01 us  [exchange(): lax.all_to_all(blocks, ('circ', 'span'), split_axis=0, concat_axis=0, til...]
  transfers between devices with their start and end apart: 16 -> 31, of which waited for: 4 -> 4; matrix products, arithmetic and copies ran while one was open for 0% -> 0% of each run, Pallas kernels for 0% -> 16%
where the time goes in v1:
time: 164 us; the launch traced here: 163 us
  blocking collectives  53.6 us (33%)
  Pallas kernels  42.4 us (26%)
  starting transfers between devices  36.1 us (22%)
  waiting for transfers between devices  23.3 us (14%)
  local copies, waits for them, and re-layouts  6.75 us (4%)
    all_to_all x1, blocking collectives, exchange(): lax.all_to_all(blocks, ('circ', 'span'), split_axis=0, concat_axis=0, til...  53.6 us
    ppermute x30, starting transfers between devices, local(): arrivals[side].append(lax.ppermute(end, 'circ', [pair]))  24.6 us
    ppermute x30, waiting for transfers between devices, local(): arrivals[side].append(lax.ppermute(end, 'circ', [pair]))  23.3 us
    pallas_call x1, Pallas kernels, local(): pl.pallas_call(bundle_kernel, out_shape=[bundle_shape] * 2, grid=(SEGMENT...  21.1 us
    all_to_all x1, starting transfers between devices, exchange(): lax.all_to_all(blocks, ('circ', 'span'), split_axis=0, concat_axis=0, til...  11.5 us
    unnamed x10, local copies, waits for them, and re-layouts  6.75 us
    pallas_call x31, Pallas kernels, sweep(): pl.pallas_call(kernel, out_shape=shape, in_specs=[IN_VMEM] * len(operands...  6.56 us
    pallas_call x1, Pallas kernels, local(): pl.pallas_call(forcing_kernel, out_shape=[forcing_shape] * 2 + [hot_shape...  6.51 us
  transfers between devices with their start and end apart: 31, of which 4 were waited for; matrix products, arithmetic and copies ran while one was open for 0% of the time, Pallas kernels for 16%

profile of v1, /device:TPU:1, one launch (start us, length us, event | category | flops | bytes accessed | tf_op | source)
XLA Modules:
  0.0 162.9 jit_solution(16273386522131207336)
XLA Ops:
  0.0 0.7 copy.12
  0.7 0.9 copy-done.2
  1.6 1.8 %pack_rows.1 = bf16[1024,128]{1,0:T(8,128)(2,1)} custom-call(bf16[80,768]{1,0:T(8,128)(2,1)S(1)} %copy-done.2, s32[12,128]{1,0:T(8,128)S(1)} %bitcast.18), custom_call_target="tpu_custom_call" | custom-call | tf_op jit(solution)/shard_map/pack_rows/pallas_call | solution.py:302
  3.4 11.5 %all-to-all-start = ((bf16[128,8,128]{2,1,0:T(8,128)(2,1)}), bf16[128,8,128]{2,1,0:T(8,128)(2,1)S(1)}, u32[]{:S(2)}, u32[]{:S(2)}) async-start(bf16[128,8,128]{2,1,0:T(8,128)(2,1)} %bitcast.2), calls=%async_computation | async-start | bytes 524288 | tf_op jit(solution)/shard_map/all_to_all | solution.py:289
  14.9 0.7 copy.11
  15.6 21.1 %bundle.1 = (bf16[6,40,80,128]{3,2,1,0:T(8,128)(2,1)S(1)}, bf16[6,40,80,128]{3,2,1,0:T(8,128)(2,1)S(1)}) custom-call(bf16[6,2,40,80,128]{4,3,2,1,0:T(8,128)(2,1)} %bitcast.21), custom_call_target="tpu_custom_call" | custom-call | bytes 19660800 | tf_op jit(solution)/shard_map/bundle/pallas_call | solution.py:313
  36.7 2.2 %copy-done = bf16[6,40,80,128]{3,2,1,0:T(8,128)(2,1)} copy-done((bf16[6,40,80,128]{3,2,1,0:T(8,128)(2,1)}, bf16[6,40,80,128]{3,2,1,0:T(8,128)(2,1)S(1)}, u32[]{:S(2)}) %copy-start) | copy-done | bytes 4915224
  38.9 2.3 %copy-done.1 = bf16[6,40,80,128]{3,2,1,0:T(8,128)(2,1)} copy-done((bf16[6,40,80,128]{3,2,1,0:T(8,128)(2,1)}, bf16[6,40,80,128]{3,2,1,0:T(8,128)(2,1)S(1)}, u32[]{:S(2)}) %copy-start.1) | copy-done | bytes 4915224
  41.2 6.5 %forcing.1 = (f32[6,40,128]{2,1,0:T(8,128)S(1)}, f32[6,40,128]{2,1,0:T(8,128)S(1)}, bf16[768,768]{1,0:T(8,128)(2,1)S(1)}, bf16[768,768]{1,0:T(8,128)(2,1)S(1)}, bf16[6,40,80,128]{3,2,1,0:T(8,128)(2,1)S(1)}) custom-call(bf16[1024,128]{1,0:T(8,128)(2,1)S(1)} %bitcast.17, s32[12,128]{1,0:T(8,128)S(1)} %bitcast.20, s32[1,128]{1,0:T(1,128)S(1)} %copy-done.3, ...), custom_call_target="tpu_custom_call" | custom-call | tf_op jit(solution)/shard_map/forcing/pallas_call | solution.py:325
  47.7 2.4 %hop_a.15 = (f32[40,128]{1,0:T(8,128)S(1)}, bf16[6,40,80,128]{3,2,1,0:T(8,128)(2,1)S(1)}) custom-call(bf16[6,40,80,128]{3,2,1,0:T(8,128)(2,1)} %copy-done, bf16[6,40,80,128]{3,2,1,0:T(8,128)(2,1)S(1)} %get-tuple-element.16.coupling_ref.refs_1_.refs_8_, f32[6,40,128]{2,1,0:T(8,128)S(1)} %get-tuple-element.17.forcing_ref.refs_2_.refs_9_), custom_call_target="tpu_custom_call" | custom-call | tf_op jit(solution)/shard_map/hop_a/pallas_call | solution.py:343
  50.1 1.0 hop_b.15
  51.1 2.3 %collective-permute-start.15 = (f32[40,128]{1,0:T(8,128)S(1)}, f32[40,128]{1,0:T(8,128)S(1)}, u32[]{:S(2)}, u32[]{:S(2)}) collective-permute-start(f32[40,128]{1,0:T(8,128)S(1)} %hop_b.15), channel_id=1, source_target_pairs={{0,16},{1,17},{2,18},{3,19},{4,20},{5,21},{6,22},{7,23},{8,24},{9,... | collective-permute-start | bytes 61448 | tf_op jit(solution)/shard_map/ppermute | solution.py:378
  53.4 1.3 collective-permute-start
  54.8 0.7 collective-permute-start.16
  56.3 0.7 collective-permute-start.17
  57.0 0.7 collective-permute-start.2
  57.7 0.7 collective-permute-start.18
  58.4 0.7 collective-permute-start.3
  59.1 0.7 collective-permute-start.19
  59.8 0.7 collective-permute-start.4
  60.6 0.7 collective-permute-start.20
  61.3 0.7 collective-permute-start.5
  62.0 0.7 collective-permute-start.21
  62.7 0.7 collective-permute-start.6
  63.4 1.3 collective-permute-start.22
  64.7 1.3 collective-permute-start.7
  66.0 22.3 %collective-permute-done.22.refs_0_ = f32[40,128]{1,0:T(8,128)S(1)} collective-permute-done((f32[40,128]{1,0:T(8,128)S(1)}, f32[40,128]{1,0:T(8,128)S(1)}, u32[]{:S(2)}, u32[]{:S(2)}) %collective-permute-start.22) | collective-permute-done | bytes 20512 | tf_op jit(solution)/shard_map/ppermute | solution.py:378
  88.3 1.2 hop_b.23
  89.6 1.3 collective-permute-start.23
  91.4 1.2 hop_a.23
  92.6 1.3 collective-permute-start.8
  94.0 0.7 collective-permute-start.24
  94.8 0.7 collective-permute-start.9
  95.5 0.7 collective-permute-start.25
  96.2 0.7 collective-permute-start.10
  96.9 0.7 collective-permute-start.26
  97.8 0.7 collective-permute-start.11
  98.5 0.7 collective-permute-start.27
  99.2 0.7 collective-permute-start.12
  99.9 0.7 collective-permute-start.28
  100.6 0.7 collective-permute-start.13
  101.3 0.7 collective-permute-start.29
  102.0 0.7 collective-permute-start.14
  102.7 1.2 final_b.1.solved_b
  104.0 1.2 final_a.1.solved_a
  105.2 1.5 return_pack.1
  106.8 53.6 %all_to_all.10 = f32[128,8,128]{2,1,0:T(8,128)S(1)} all-to-all(f32[128,8,128]{2,1,0:T(8,128)S(1)} %bitcast.16), channel_id=1, replica_groups=mesh['circ'=8,'span'=16] {'circ','span'}, dimensions={0} | all-to-all | bytes 1048576 | tf_op jit(solution)/shard_map/all_to_all | solution.py:289
  160.4 2.5 %return_rows.1 = f32[80,768]{1,0:T(8,128)} custom-call(f32[1024,128]{1,0:T(8,128)S(1)} %bitcast.15, s32[12,128]{1,0:T(8,128)S(1)} %bitcast.19), custom_call_target="tpu_custom_call" | custom-call | tf_op jit(solution)/shard_map/return_rows/pallas_call | solution.py:393
  (62 shorter events, 2.2 us)
Async XLA Ops:
  0.7 0.9 copy-start.2
  3.4 37.7 %all-to-all-start = ((bf16[128,8,128]{2,1,0:T(8,128)(2,1)}), bf16[128,8,128]{2,1,0:T(8,128)(2,1)S(1)}, u32[]{:S(2)}, u32[]{:S(2)}) async-start(bf16[128,8,128]{2,1,0:T(8,128)(2,1)} %bitcast.2), calls=%async_computation | async-start | bytes 524288 | tf_op jit(solution)/shard_map/all_to_all | solution.py:289
  15.6 25.6 %copy-start.3 = (s32[1,128]{1,0:T(1,128)S(1)}, s32[1,128]{1,0:T(1,128)}, u32[]{:S(2)}) copy-start(s32[1,128]{1,0:T(1,128)} %counts_ref.1) | copy-start | bytes 1540
  36.7 2.2 %copy-start = (bf16[6,40,80,128]{3,2,1,0:T(8,128)(2,1)}, bf16[6,40,80,128]{3,2,1,0:T(8,128)(2,1)S(1)}, u32[]{:S(2)}) copy-start(bf16[6,40,80,128]{3,2,1,0:T(8,128)(2,1)S(1)} %get-tuple-element.14.bundle_hbm) | copy-start | bytes 14745604
  38.9 2.3 %copy-start.1 = (bf16[6,40,80,128]{3,2,1,0:T(8,128)(2,1)}, bf16[6,40,80,128]{3,2,1,0:T(8,128)(2,1)S(1)}, u32[]{:S(2)}) copy-start(bf16[6,40,80,128]{3,2,1,0:T(8,128)(2,1)S(1)} %get-tuple-element.15.bundle_hbm) | copy-start | bytes 14745604
  51.1 3.6 %collective-permute-start.15 = (f32[40,128]{1,0:T(8,128)S(1)}, f32[40,128]{1,0:T(8,128)S(1)}, u32[]{:S(2)}, u32[]{:S(2)}) collective-permute-start(f32[40,128]{1,0:T(8,128)S(1)} %hop_b.15), channel_id=1, source_target_pairs={{0,16},{1,17},{2,18},{3,19},{4,20},{5,21},{6,22},{7,23},{8,24},{9,... | collective-permute-start | bytes 61448 | tf_op jit(solution)/shard_map/ppermute | solution.py:378
  53.4 2.2 %collective-permute-start = (f32[40,128]{1,0:T(8,128)S(1)}, f32[40,128]{1,0:T(8,128)S(1)}, u32[]{:S(2)}, u32[]{:S(2)}) collective-permute-start(f32[40,128]{1,0:T(8,128)S(1)} %get-tuple-element.18), channel_id=1, source_target_pairs={{0,16},{1,17},{2,18},{3,19},{4,20},{5,21},{6,22},{7,23},{8,24},{9,... | collective-permute-start | bytes 61448 | tf_op jit(solution)/shard_map/ppermute | solution.py:378
  54.8 1.5 collective-permute-start.16
  55.6 1.4 collective-permute-start.1
  56.3 1.4 collective-permute-start.17
  57.0 1.4 collective-permute-start.2
  57.7 1.4 collective-permute-start.18
  58.4 1.4 collective-permute-start.3
  59.1 1.4 collective-permute-start.19
  59.8 1.4 collective-permute-start.4
  60.6 1.4 collective-permute-start.20
  61.3 1.4 collective-permute-start.5
  62.0 1.4 collective-permute-start.21
  62.7 2.0 %collective-permute-start.6 = (f32[40,128]{1,0:T(8,128)S(1)}, f32[40,128]{1,0:T(8,128)S(1)}, u32[]{:S(2)}, u32[]{:S(2)}) collective-permute-start(f32[40,128]{1,0:T(8,128)S(1)} %hop_a.21), channel_id=1, source_target_pairs={{96,112},{97,113},{98,114},{99,115},{100,116},{101,117},{102,118},... | collective-permute-start | bytes 61448 | tf_op jit(solution)/shard_map/ppermute | solution.py:378
  63.4 24.9 %collective-permute-start.22 = (f32[40,128]{1,0:T(8,128)S(1)}, f32[40,128]{1,0:T(8,128)S(1)}, u32[]{:S(2)}, u32[]{:S(2)}) collective-permute-start(f32[40,128]{1,0:T(8,128)S(1)} %hop_b.22), channel_id=1, source_target_pairs={{112,0},{113,1},{114,2},{115,3},{116,4},{117,5},{118,6},{119,7},{1... | collective-permute-start | bytes 61448 | tf_op jit(solution)/shard_map/ppermute | solution.py:378
  64.7 26.7 %collective-permute-start.7 = (f32[40,128]{1,0:T(8,128)S(1)}, f32[40,128]{1,0:T(8,128)S(1)}, u32[]{:S(2)}, u32[]{:S(2)}) collective-permute-start(f32[40,128]{1,0:T(8,128)S(1)} %hop_a.22), channel_id=1, source_target_pairs={{112,0},{113,1},{114,2},{115,3},{116,4},{117,5},{118,6},{119,7},{1... | collective-permute-start | bytes 61448 | tf_op jit(solution)/shard_map/ppermute | solution.py:378
  89.6 4.4 %collective-permute-start.23 = (f32[40,128]{1,0:T(8,128)S(1)}, f32[40,128]{1,0:T(8,128)S(1)}, u32[]{:S(2)}, u32[]{:S(2)}) collective-permute-start(f32[40,128]{1,0:T(8,128)S(1)} %hop_b.23), channel_id=1, source_target_pairs={{0,16},{1,17},{2,18},{3,19},{4,20},{5,21},{6,22},{7,23},{8,24},{9,... | collective-permute-start | bytes 61448 | tf_op jit(solution)/shard_map/ppermute | solution.py:378
  92.6 2.2 %collective-permute-start.8 = (f32[40,128]{1,0:T(8,128)S(1)}, f32[40,128]{1,0:T(8,128)S(1)}, u32[]{:S(2)}, u32[]{:S(2)}) collective-permute-start(f32[40,128]{1,0:T(8,128)S(1)} %hop_a.23), channel_id=1, source_target_pairs={{0,16},{1,17},{2,18},{3,19},{4,20},{5,21},{6,22},{7,23},{8,24},{9,... | collective-permute-start | bytes 61448 | tf_op jit(solution)/shard_map/ppermute | solution.py:378
  94.0 1.5 collective-permute-start.24
  94.8 1.4 collective-permute-start.9
  95.5 1.4 collective-permute-start.25
  96.2 1.4 collective-permute-start.10
  96.9 1.6 collective-permute-start.26
  97.8 1.4 collective-permute-start.11
  98.5 1.4 collective-permute-start.27
  99.2 1.4 collective-permute-start.12
  99.9 1.4 collective-permute-start.28
  100.6 1.4 collective-permute-start.13
  101.3 1.4 collective-permute-start.29
  102.0 1.9 %collective-permute-start.14 = (f32[40,128]{1,0:T(8,128)S(1)}, f32[40,128]{1,0:T(8,128)S(1)}, u32[]{:S(2)}, u32[]{:S(2)}) collective-permute-start(f32[40,128]{1,0:T(8,128)S(1)} %hop_a.29), channel_id=1, source_target_pairs={{96,112},{97,113},{98,114},{99,115},{100,116},{101,117},{102,118},... | collective-permute-start | bytes 61448 | tf_op jit(solution)/shard_map/ppermute | solution.py:378

commit v2 on v1

--- a/solution.py
+++ b/solution.py
@@ -149,32 +149,56 @@
     return total[:FEATURES]
 
 
-def pack_rows_kernel(rows_ref, send_ref, out_ref, wide):
+def pack_rows_kernel(rows_hbm, send_ref, out_ref, wide, rows_ref, sem):
+    copy = pltpu.make_async_copy(rows_hbm, rows_ref, sem)
+    copy.start()
+
     def store(r, block):
         wide[pl.ds(r, PEERS, stride=ROWS), :] = block
 
-    index = columns(send_ref[...])
-    pack([rows_ref[...]], (one_hot(index, 0), one_hot(index, 1)), store)
+    index = columns(send_ref[...].reshape(SLOTS, PEERS))
+    hots = one_hot(index, 0), one_hot(index, 1)
+    copy.wait()
+    pack([rows_ref[...]], hots, store)
     out_ref[...] = wide[...].astype(BF16)
 
 
 def bundle_kernel(coupling_ref, bundle_a, bundle_b):
+    on_left = left(FEATURES)
+
+    @pl.loop(0, coupling_ref.shape[2], unroll=4)
+    def _(i):
+        low = coupling_ref[0, 0, i]
+        high = swap(coupling_ref[0, 1, i].astype(F32)).astype(BF16)
+        bundle_a[0, i] = jnp.where(on_left, low, high)
+        bundle_b[0, i] = jnp.where(on_left, high, low)
+
+
+def advance(side, coupling_ref, forcing_ref, first, state, record=None):
+    row = sublane_ids()
     on_left = left(HALF)
 
-    @pl.loop(0, coupling_ref.shape[2])
-    def _(i):
-        low = coupling_ref[0, 0, i].astype(F32)
-        high = coupling_ref[0, 1, i].astype(F32)
-        for ref, a, b in ((bundle_a, low, swap(high)), (bundle_b, swap(low), high)):
-            same = jnp.where(on_left, a[:HALF], b[HALF:])
-            cross = jnp.where(on_left, a[HALF:], b[:HALF])
-            ref[0, i] = jnp.concatenate([same, cross], axis=0).astype(BF16)
+    def step(position, state):
+        moved = swap(state)
+        both = [jnp.where(on_left, state, moved), jnp.where(on_left, moved, state)]
+        both = jnp.concatenate(both[::-1] if side else both, axis=0)
+        state = forcing_ref[position] + matvec(coupling_ref, position, both, row)
+        if record is not None:
+            record[position] = state
+        return state
+
+    if callable(first):
+        for position in range(1, SEGMENT):
+            first(position)
+            state = step(position, state)
+        return state
+    return lax.fori_loop(first, SEGMENT, step, state)
 
 
 def forcing_kernel(
     arrived_ref, cells_ref, counts_ref, inverses_hbm, bundle_hbm,
-    forcing_a, forcing_b, even_ref, odd_ref, bundle_ref,
-    wide, lines, inverses_ref, sems, bundle_sem,
+    forcing_a, forcing_b, even_ref, odd_ref, bundle_ref, end_ref,
+    wide, lines, inverses_ref, sems, bundle_sems,
 ):
     copies = [
         pltpu.make_async_copy(inverses_hbm.at[p], inverses_ref.at[p], sems.at[p])
@@ -182,11 +206,15 @@
     ]
     for copy in copies:
         copy.start()
-    bundle_copy = pltpu.make_async_copy(bundle_hbm, bundle_ref, bundle_sem)
-    bundle_copy.start()
+    bundle_copies = [
+        pltpu.make_async_copy(bundle_hbm.at[p], bundle_ref.at[p], bundle_sems.at[p])
+        for p in range(SEGMENT)
+    ]
+    for copy in bundle_copies[1:] + bundle_copies[:1]:
+        copy.start()
     wide[...] = arrived_ref[...].astype(F32)
     slot = lax.broadcasted_iota(jnp.int32, (SLOTS, PEERS), 0)
-    index = columns(jnp.where(slot < counts_ref[...], cells_ref[...], -1))
+    index = columns(jnp.where(slot < counts_ref[...], cells_ref[...].reshape(SLOTS, PEERS), -1))
     hots = one_hot(index, 0), one_hot(index, 1)
     even_ref[...], odd_ref[...] = hots
     found = unpack(lambda r: wide[pl.ds(r, PEERS, stride=ROWS), :], hots, 1)
@@ -197,57 +225,42 @@
     for p in range(SEGMENT):
         copies[p].wait()
         forcing = matvec(inverses_ref, p, lines[p], row)
-        low, high = forcing[:HALF], forcing[HALF:]
-        forcing_a[p] = jnp.where(on_left, low, swap(high))
-        forcing_b[p] = jnp.where(on_left, swap(low), high)
-    bundle_copy.wait()
-
-
-def advance(coupling_ref, forcing_ref, first, state, record=None):
-    row = sublane_ids()
-
-    def step(position, state):
-        both = jnp.concatenate([state, swap(state)], axis=0)
-        state = forcing_ref[position] + matvec(coupling_ref, position, both, row)
-        if record is not None:
-            record[position] = state
-        return state
-
-    return lax.fori_loop(first, SEGMENT, step, state)
+        low, high = forcing[:HALF], swap(forcing[HALF:])
+        forcing_a[p] = jnp.where(on_left, low, high)
+        forcing_b[p] = jnp.where(on_left, high, low)
+    end_ref[...] = advance(
+        0, bundle_ref, forcing_a, lambda p: bundle_copies[p].wait(), forcing_a[0]
+    )
+    bundle_copies[0].wait()
 
 
 def here(hop):
     return lax.axis_index("circ") == hop % N_CIRC
 
 
-def first_hop_kernel(bundle_hbm, coupling_ref, forcing_ref, end_ref, bundle_ref, sem):
-    copy = pltpu.make_async_copy(bundle_hbm, bundle_ref, sem)
-    copy.start()
-
-    @pl.when(here(0))
-    def _():
-        end_ref[...] = advance(coupling_ref, forcing_ref, 1, forcing_ref[0])
-
-    copy.wait()
-
-
-def hop_kernel(hop, *refs):
-    *state_refs, coupling_ref, forcing_ref, end_ref = refs
-
+def first_hop_kernel(bundle_hbm, forcing_ref, end_ref, bundle_ref, sems):
+    copies = [
+        pltpu.make_async_copy(bundle_hbm.at[p], bundle_ref.at[p], sems.at[p])
+        for p in range(SEGMENT)
+    ]
+    for copy in copies[1:] + copies[:1]:
+        copy.start()
+    end_ref[...] = advance(1, bundle_ref, forcing_ref, lambda p: copies[p].wait(), forcing_ref[0])
+    copies[0].wait()
+
+
+def hop_kernel(hop, side, state_ref, coupling_ref, forcing_ref, end_ref):
     @pl.when(here(hop))
     def _():
-        if state_refs:
-            end_ref[...] = advance(coupling_ref, forcing_ref, 0, state_refs[0][...])
-        else:
-            end_ref[...] = advance(coupling_ref, forcing_ref, 1, forcing_ref[0])
-
-
-def final_kernel(*refs):
+        end_ref[...] = advance(side, coupling_ref, forcing_ref, 0, state_ref[...])
+
+
+def final_kernel(side, *refs):
     *state_refs, coupling_ref, forcing_ref, solved_ref = refs
     state = state_refs[0][...]
     for ref in state_refs[1:]:
         state = state + ref[...]
-    advance(coupling_ref, forcing_ref, 0, state, solved_ref)
+    advance(side, coupling_ref, forcing_ref, 0, state, solved_ref)
 
 
 def return_pack_kernel(solved_a, solved_b, even_ref, odd_ref, out_ref):
@@ -258,8 +271,8 @@
     cells = []
     for position in range(SEGMENT):
         a, b = solved_a[position], solved_b[position]
-        low = jnp.where(on_left, a, swap(b))
-        high = jnp.where(on_left, swap(a), b)
+        low = jnp.where(on_left, a, b)
+        high = swap(jnp.where(on_left, b, a))
         cells.append(jnp.concatenate([low, high], axis=0))
     rest = jnp.concatenate(cells, axis=1)
     high = rest.astype(BF16)
@@ -268,7 +281,7 @@
 
 
 def return_kernel(arrived_ref, send_ref, out_ref):
-    index = columns(send_ref[...])
+    index = columns(send_ref[...].reshape(SLOTS, PEERS))
     out_ref[...] = unpack(
         lambda r: arrived_ref[pl.ds(r, PEERS, stride=ROWS), :],
         (one_hot(index, 0), one_hot(index, 1)),
@@ -291,8 +304,8 @@
 
 
 def local(elem_rows, coupling, inverses, send_rows, recv_cells, slot_counts):
-    send = jnp.transpose(send_rows[0])
-    cells = jnp.transpose(recv_cells[0])
+    send = jnp.transpose(send_rows, (2, 0, 1))
+    cells = jnp.transpose(recv_cells, (2, 0, 1))
     packed_rows = (PEERS * ROWS, LANES)
     hot_shape = jax.ShapeDtypeStruct((PAIRS * PEERS, CELLS), BF16)
     bundle_shape = jax.ShapeDtypeStruct((SEGMENT, HALF, FEATURES, LANES), BF16)
@@ -302,17 +315,21 @@
     outgoing = pl.pallas_call(
         pack_rows_kernel,
         out_shape=jax.ShapeDtypeStruct(packed_rows, BF16),
-        in_specs=[IN_VMEM] * 2,
+        in_specs=[in_hbm, IN_VMEM],
         out_specs=IN_VMEM,
-        scratch_shapes=[pltpu.VMEM(packed_rows, F32)],
+        scratch_shapes=[
+            pltpu.VMEM(packed_rows, F32),
+            pltpu.VMEM(elem_rows.shape, BF16),
+            pltpu.SemaphoreType.DMA,
+        ],
         compiler_params=params(16),
         name="pack_rows",
-    )(elem_rows, send)
+    )(hbm(elem_rows), send)
     arrived = exchange(outgoing)
     split = 2
     bundles = pl.pallas_call(
         bundle_kernel,
-        out_shape=[bundle_shape] * 2,
+        out_shape=[pltpu.HBM(bundle_shape.shape, BF16)] * 2,
         grid=(SEGMENT, split),
         in_specs=[
             pl.BlockSpec((1, 2, HALF // split, FEATURES, LANES), lambda p, k: (p, 0, k, 0, 0))
@@ -322,34 +339,33 @@
         cost_estimate=pl.CostEstimate(flops=0, bytes_accessed=4 * coupling.size, transcendentals=0),
         name="bundle",
     )(hbm(coupling.reshape(SEGMENT, 2, HALF, FEATURES, LANES)))
-    *forcings, even, odd, bundle_a = pl.pallas_call(
+    *forcings, even, odd, bundle_a, end_a = pl.pallas_call(
         forcing_kernel,
-        out_shape=[forcing_shape] * 2 + [hot_shape] * 2 + [bundle_shape],
+        out_shape=[forcing_shape] * 2 + [hot_shape] * 2 + [bundle_shape, state_shape],
         in_specs=[IN_VMEM] * 3 + [in_hbm] * 2,
-        out_specs=[IN_VMEM] * 5,
+        out_specs=[IN_VMEM] * 6,
         scratch_shapes=[
             pltpu.VMEM(packed_rows, F32),
             pltpu.VMEM((SEGMENT, FEATURES, LINES), F32),
             pltpu.VMEM(inverses.shape, BF16),
             pltpu.SemaphoreType.DMA((SEGMENT,)),
-            pltpu.SemaphoreType.DMA,
+            pltpu.SemaphoreType.DMA((SEGMENT,)),
         ],
         compiler_params=params(24),
         name="forcing",
     )(arrived, cells, slot_counts, hbm(inverses), hbm(bundles[0]))
     even, odd = vmem(even), vmem(odd)
-    bundle_a = vmem(bundle_a)
     forcings = [vmem(forcing) for forcing in forcings]
-    end_a, bundle_b = pl.pallas_call(
+    end_b, bundle_b = pl.pallas_call(
         first_hop_kernel,
         out_shape=[state_shape, bundle_shape],
-        in_specs=[in_hbm] + [IN_VMEM] * 2,
+        in_specs=[in_hbm, IN_VMEM],
         out_specs=[IN_VMEM] * 2,
-        scratch_shapes=[pltpu.SemaphoreType.DMA],
+        scratch_shapes=[pltpu.SemaphoreType.DMA((SEGMENT,))],
         compiler_params=params(8),
-        name="hop_a",
-    )(hbm(bundles[1]), bundle_a, forcings[0])
-    bundles = [bundle_a, vmem(bundle_b)]
+        name="first_hop",
+    )(hbm(bundles[1]), forcings[1])
+    bundles = [vmem(bundle_a), vmem(bundle_b)]
 
     def sweep(side, kernel, states, shape, name):
         operands = [*states, bundles[side], forcings[side]]
@@ -368,16 +384,14 @@
     arrivals = ([], [])
     for hop in range(2 * N_CIRC - 1):
         for side in range(2):
-            if hop == 0 and side == 0:
-                end = end_a
-            else:
-                end = sweep(
-                    side, functools.partial(hop_kernel, hop), arrivals[side][-1:], state_shape, "hop_"
-                )
+            end = (end_a, end_b)[side]
+            if hop:
+                kernel = functools.partial(hop_kernel, hop, side)
+                end = sweep(side, kernel, arrivals[side][-1:], state_shape, "hop_")
             pair = (hop % N_CIRC, (hop + 1) % N_CIRC)
             arrivals[side].append(lax.ppermute(end, "circ", [pair]))
     solved = [
-        sweep(side, final_kernel, arrivals[side][N_CIRC - 1 :], forcing_shape, "final_")
+        sweep(side, functools.partial(final_kernel, side), arrivals[side][N_CIRC - 1 :], forcing_shape, "final_")
         for side in range(2)
     ]
 

time: 164 us -> 156 us (0.951)
  local copies, waits for them, and re-layouts: 6.75 us -> 0.71 us
  Pallas kernels: 42.4 us -> 36.7 us
  blocking collectives: 53.6 us -> 55.4 us
    pallas_call x1, Pallas kernels: 21.1 us -> 13.3 us  [local(): pl.pallas_call(bundle_kernel, out_shape=[pltpu.HBM(bundle_shape.shape, BF...]
    unnamed x10 -> x8, local copies, waits for them, and re-layouts: 6.75 us -> 0.71 us
    all_to_all x1, blocking collectives: 53.6 us -> 55.4 us  [exchange(): lax.all_to_all(blocks, ('circ', 'span'), split_axis=0, concat_axis=0, til...]
    pallas_call x31 -> x30, Pallas kernels: 6.56 us -> 6.68 us  [sweep(): pl.pallas_call(kernel, out_shape=shape, in_specs=[IN_VMEM] * len(operands...]
  transfers between devices with their start and end apart: 31 -> 31, of which waited for: 4 -> 3; matrix products, arithmetic and copies ran while one was open for 0% -> 0% of each run, Pallas kernels for 16% -> 12%
where the time goes in v2:
time: 156 us; the launch traced here: 155 us
  blocking collectives  55.4 us (36%)
  starting transfers between devices  37.1 us (24%)
  Pallas kernels  36.7 us (24%)
  waiting for transfers between devices  24.6 us (16%)
    all_to_all x1, blocking collectives, exchange(): lax.all_to_all(blocks, ('circ', 'span'), split_axis=0, concat_axis=0, til...  55.4 us
    ppermute x30, starting transfers between devices, local(): arrivals[side].append(lax.ppermute(end, 'circ', [pair]))  25.6 us
    ppermute x30, waiting for transfers between devices, local(): arrivals[side].append(lax.ppermute(end, 'circ', [pair]))  24.6 us
    pallas_call x1, Pallas kernels, local(): pl.pallas_call(bundle_kernel, out_shape=[pltpu.HBM(bundle_shape.shape, BF...  13.3 us
    all_to_all x1, starting transfers between devices, exchange(): lax.all_to_all(blocks, ('circ', 'span'), split_axis=0, concat_axis=0, til...  11.5 us
    pallas_call x1, Pallas kernels, local(): pl.pallas_call(forcing_kernel, out_shape=[forcing_shape] * 2 + [hot_shape...  7.74 us
    pallas_call x30, Pallas kernels, sweep(): pl.pallas_call(kernel, out_shape=shape, in_specs=[IN_VMEM] * len(operands...  6.68 us
  transfers between devices with their start and end apart: 31, of which 3 were waited for; matrix products, arithmetic and copies ran while one was open for 0% of the time, Pallas kernels for 12%

profile of v2, /device:TPU:1, one launch (start us, length us, event | category | flops | bytes accessed | tf_op | source)
XLA Modules:
  0.0 155.2 jit_solution(2858532671596606523)
XLA Ops:
  0.0 0.7 copy-done
  0.7 2.5 %pack_rows.1 = bf16[1024,128]{1,0:T(8,128)(2,1)} custom-call(bf16[80,768]{1,0:T(8,128)(2,1)} %rows_hbm.1, s32[12,1,128]{2,1,0:T(1,128)S(1)} %bitcast.10), custom_call_target="tpu_custom_call" | custom-call | tf_op jit(solution)/shard_map/pack_rows/pallas_call | solution.py:315
  3.2 11.5 %all-to-all-start = ((bf16[128,8,128]{2,1,0:T(8,128)(2,1)}), bf16[128,8,128]{2,1,0:T(8,128)(2,1)S(1)}, u32[]{:S(2)}, u32[]{:S(2)}) async-start(bf16[128,8,128]{2,1,0:T(8,128)(2,1)} %bitcast.1), calls=%async_computation | async-start | bytes 524288 | tf_op jit(solution)/shard_map/all_to_all | solution.py:302
  14.7 13.3 %bundle.1 = (bf16[6,40,80,128]{3,2,1,0:T(8,128)(2,1)}, bf16[6,40,80,128]{3,2,1,0:T(8,128)(2,1)}) custom-call(bf16[6,2,40,80,128]{4,3,2,1,0:T(8,128)(2,1)} %bitcast.13), custom_call_target="tpu_custom_call" | custom-call | bytes 19660800 | tf_op jit(solution)/shard_map/bundle/pallas_call | solution.py:330
  28.0 7.7 %forcing.1 = (f32[6,40,128]{2,1,0:T(8,128)S(1)}, f32[6,40,128]{2,1,0:T(8,128)S(1)}, bf16[768,768]{1,0:T(8,128)(2,1)S(1)}, bf16[768,768]{1,0:T(8,128)(2,1)S(1)}, ...) custom-call(bf16[1024,128]{1,0:T(8,128)(2,1)S(1)} %bitcast.9, s32[12,1,128]{2,1,0:T(1,128)S(1)} %bitcast.12, ...), custom_call_target="tpu_custom_call" | custom-call | tf_op jit(solution)/shard_map/forcing/pallas_call | solution.py:342
  35.8 2.5 %first_hop.1 = (f32[40,128]{1,0:T(8,128)S(1)}, bf16[6,40,80,128]{3,2,1,0:T(8,128)(2,1)S(1)}) custom-call(bf16[6,40,80,128]{3,2,1,0:T(8,128)(2,1)} %get-tuple-element.19.bundle_hbm, f32[6,40,128]{2,1,0:T(8,128)S(1)} %get-tuple-element.20.forcing_ref.refs_9_), custom_call_target="tpu_custom_call" | custom-call | tf_op jit(solution)/shard_map/first_hop/pallas_call | solution.py:359
  38.2 3.3 %collective-permute-start.15 = (f32[40,128]{1,0:T(8,128)S(1)}, f32[40,128]{1,0:T(8,128)S(1)}, u32[]{:S(2)}, u32[]{:S(2)}) collective-permute-start(f32[40,128]{1,0:T(8,128)S(1)} %get-tuple-element.21), channel_id=1, source_target_pairs={{0,16},{1,17},{2,18},{3,19},{4,20},{5,21},{6,22},{7,23},{8,24},{9,... | collective-permute-start | bytes 61448 | tf_op jit(solution)/shard_map/ppermute | solution.py:392
  41.5 1.3 collective-permute-start
  42.9 0.7 collective-permute-start.16
  43.6 0.2 collective-permute-done.state_ref
  43.7 0.7 collective-permute-start.1
  44.4 0.7 collective-permute-start.17
  45.1 0.7 collective-permute-start.2
  45.8 0.7 collective-permute-start.18
  46.5 0.7 collective-permute-start.3
  47.3 0.7 collective-permute-start.19
  48.0 0.7 collective-permute-start.4
  48.7 0.7 collective-permute-start.20
  49.4 0.7 collective-permute-start.5
  50.1 0.7 collective-permute-start.21
  50.8 0.7 collective-permute-start.6
  51.5 0.2 hop_b.20
  51.7 1.3 collective-permute-start.22
  53.0 1.3 collective-permute-start.7
  54.3 24.2 %collective-permute-done.22.state_ref.refs_0_ = f32[40,128]{1,0:T(8,128)S(1)} collective-permute-done((f32[40,128]{1,0:T(8,128)S(1)}, f32[40,128]{1,0:T(8,128)S(1)}, u32[]{:S(2)}, u32[]{:S(2)}) %collective-permute-start.22) | collective-permute-done | bytes 20512 | tf_op jit(solution)/shard_map/ppermute | solution.py:392
  78.5 1.5 hop_b.21
  80.0 1.3 collective-permute-start.23
  81.3 0.0 collective-permute-done.7.state_ref.refs_0_
  81.3 1.5 hop_a.21
  82.8 1.3 collective-permute-start.8
  84.2 0.7 collective-permute-start.24
  84.8 0.2 collective-permute-done.8.state_ref.refs_1_
  85.0 0.7 collective-permute-start.9
  85.7 0.7 collective-permute-start.25
  86.4 0.7 collective-permute-start.10
  87.1 0.7 collective-permute-start.26
  87.8 0.7 collective-permute-start.11
  88.5 0.7 collective-permute-start.27
  89.2 0.7 collective-permute-start.12
  90.0 0.7 collective-permute-start.28
  90.7 0.7 collective-permute-start.13
  91.4 0.7 collective-permute-start.29
  92.1 0.7 collective-permute-start.14
  92.8 1.5 final_b.1.solved_b
  94.3 1.5 final_a.1.solved_a
  95.9 1.5 return_pack.1
  97.4 55.4 %all_to_all.10 = f32[128,8,128]{2,1,0:T(8,128)S(1)} all-to-all(f32[128,8,128]{2,1,0:T(8,128)S(1)} %bitcast.8), channel_id=1, replica_groups=mesh['circ'=8,'span'=16] {'circ','span'}, dimensions={0} | all-to-all | bytes 1048576 | tf_op jit(solution)/shard_map/all_to_all | solution.py:302
  152.7 2.5 %return_rows.1 = f32[80,768]{1,0:T(8,128)} custom-call(f32[1024,128]{1,0:T(8,128)S(1)} %bitcast.7, s32[12,1,128]{2,1,0:T(1,128)S(1)} %bitcast.11), custom_call_target="tpu_custom_call" | custom-call | tf_op jit(solution)/shard_map/return_rows/pallas_call | solution.py:407
  (59 shorter events, 0.5 us)
Async XLA Ops:
  0.0 0.7 copy-start
  3.2 24.8 %all-to-all-start = ((bf16[128,8,128]{2,1,0:T(8,128)(2,1)}), bf16[128,8,128]{2,1,0:T(8,128)(2,1)S(1)}, u32[]{:S(2)}, u32[]{:S(2)}) async-start(bf16[128,8,128]{2,1,0:T(8,128)(2,1)} %bitcast.1), calls=%async_computation | async-start | bytes 524288 | tf_op jit(solution)/shard_map/all_to_all | solution.py:302
  14.7 13.3 %copy-start.2 = (s32[1,128,12]{1,0,2:T(1,128)S(1)}, s32[1,128,12]{1,0,2:T(1,128)}, u32[]{:S(2)}) copy-start(s32[1,128,12]{1,0,2:T(1,128)} %param.10) | copy-start | bytes 18436
  14.7 13.3 %copy-start.3 = (s32[1,128]{1,0:T(1,128)S(1)}, s32[1,128]{1,0:T(1,128)}, u32[]{:S(2)}) copy-start(s32[1,128]{1,0:T(1,128)} %counts_ref.1) | copy-start | bytes 1540
  38.2 4.6 %collective-permute-start.15 = (f32[40,128]{1,0:T(8,128)S(1)}, f32[40,128]{1,0:T(8,128)S(1)}, u32[]{:S(2)}, u32[]{:S(2)}) collective-permute-start(f32[40,128]{1,0:T(8,128)S(1)} %get-tuple-element.21), channel_id=1, source_target_pairs={{0,16},{1,17},{2,18},{3,19},{4,20},{5,21},{6,22},{7,23},{8,24},{9,... | collective-permute-start | bytes 61448 | tf_op jit(solution)/shard_map/ppermute | solution.py:392
  41.5 2.2 %collective-permute-start = (f32[40,128]{1,0:T(8,128)S(1)}, f32[40,128]{1,0:T(8,128)S(1)}, u32[]{:S(2)}, u32[]{:S(2)}) collective-permute-start(f32[40,128]{1,0:T(8,128)S(1)} %get-tuple-element.16), channel_id=1, source_target_pairs={{0,16},{1,17},{2,18},{3,19},{4,20},{5,21},{6,22},{7,23},{8,24},{9,... | collective-permute-start | bytes 61448 | tf_op jit(solution)/shard_map/ppermute | solution.py:392
  42.9 1.5 collective-permute-start.16
  43.7 1.4 collective-permute-start.1
  44.4 1.4 collective-permute-start.17
  45.1 1.4 collective-permute-start.2
  45.8 1.4 collective-permute-start.18
  46.5 1.4 collective-permute-start.3
  47.3 1.4 collective-permute-start.19
  48.0 1.4 collective-permute-start.4
  48.7 1.4 collective-permute-start.20
  49.4 1.4 collective-permute-start.5
  50.1 1.4 collective-permute-start.21
  50.8 2.2 %collective-permute-start.6 = (f32[40,128]{1,0:T(8,128)S(1)}, f32[40,128]{1,0:T(8,128)S(1)}, u32[]{:S(2)}, u32[]{:S(2)}) collective-permute-start(f32[40,128]{1,0:T(8,128)S(1)} %hop_a.19), channel_id=1, source_target_pairs={{96,112},{97,113},{98,114},{99,115},{100,116},{101,117},{102,118},... | collective-permute-start | bytes 61448 | tf_op jit(solution)/shard_map/ppermute | solution.py:392
  51.7 26.8 %collective-permute-start.22 = (f32[40,128]{1,0:T(8,128)S(1)}, f32[40,128]{1,0:T(8,128)S(1)}, u32[]{:S(2)}, u32[]{:S(2)}) collective-permute-start(f32[40,128]{1,0:T(8,128)S(1)} %hop_b.20), channel_id=1, source_target_pairs={{112,0},{113,1},{114,2},{115,3},{116,4},{117,5},{118,6},{119,7},{1... | collective-permute-start | bytes 61448 | tf_op jit(solution)/shard_map/ppermute | solution.py:392
  53.0 28.3 %collective-permute-start.7 = (f32[40,128]{1,0:T(8,128)S(1)}, f32[40,128]{1,0:T(8,128)S(1)}, u32[]{:S(2)}, u32[]{:S(2)}) collective-permute-start(f32[40,128]{1,0:T(8,128)S(1)} %hop_a.20), channel_id=1, source_target_pairs={{112,0},{113,1},{114,2},{115,3},{116,4},{117,5},{118,6},{119,7},{1... | collective-permute-start | bytes 61448 | tf_op jit(solution)/shard_map/ppermute | solution.py:392
  80.0 4.2 %collective-permute-start.23 = (f32[40,128]{1,0:T(8,128)S(1)}, f32[40,128]{1,0:T(8,128)S(1)}, u32[]{:S(2)}, u32[]{:S(2)}) collective-permute-start(f32[40,128]{1,0:T(8,128)S(1)} %hop_b.21), channel_id=1, source_target_pairs={{0,16},{1,17},{2,18},{3,19},{4,20},{5,21},{6,22},{7,23},{8,24},{9,... | collective-permute-start | bytes 61448 | tf_op jit(solution)/shard_map/ppermute | solution.py:392
  82.8 2.2 %collective-permute-start.8 = (f32[40,128]{1,0:T(8,128)S(1)}, f32[40,128]{1,0:T(8,128)S(1)}, u32[]{:S(2)}, u32[]{:S(2)}) collective-permute-start(f32[40,128]{1,0:T(8,128)S(1)} %hop_a.21), channel_id=1, source_target_pairs={{0,16},{1,17},{2,18},{3,19},{4,20},{5,21},{6,22},{7,23},{8,24},{9,... | collective-permute-start | bytes 61448 | tf_op jit(solution)/shard_map/ppermute | solution.py:392
  84.2 1.5 collective-permute-start.24
  85.0 1.4 collective-permute-start.9
  85.7 1.4 collective-permute-start.25
  86.4 1.4 collective-permute-start.10
  87.1 1.4 collective-permute-start.26
  87.8 1.4 collective-permute-start.11
  88.5 1.4 collective-permute-start.27
  89.2 1.4 collective-permute-start.12
  90.0 1.4 collective-permute-start.28
  90.7 1.4 collective-permute-start.13
  91.4 1.4 collective-permute-start.29
  92.1 2.2 %collective-permute-start.14 = (f32[40,128]{1,0:T(8,128)S(1)}, f32[40,128]{1,0:T(8,128)S(1)}, u32[]{:S(2)}, u32[]{:S(2)}) collective-permute-start(f32[40,128]{1,0:T(8,128)S(1)} %hop_a.27), channel_id=1, source_target_pairs={{96,112},{97,113},{98,114},{99,115},{100,116},{101,117},{102,118},... | collective-permute-start | bytes 61448 | tf_op jit(solution)/shard_map/ppermute | solution.py:392
  94.3 58.5 %copy-start.1 = (s32[1,128,12]{1,0,2:T(1,128)S(1)}, s32[1,128,12]{1,0,2:T(1,128)}, u32[]{:S(2)}) copy-start(s32[1,128,12]{1,0,2:T(1,128)} %param.9) | copy-start | bytes 18436

commit v3 on v2

--- a/solution.py
+++ b/solution.py
@@ -54,7 +54,7 @@
         for k in range(8):
             terms = blocks_ref[position, group * 8 + k].astype(F32) * vector
             total = terms[0:8]
-            for j in range(8, FEATURES, 8):
+            for j in (*range(16, FEATURES, 16), *range(8, FEATURES, 16)):
                 total = total + terms[j : j + 8]
             parts.append(total)
         result.append(fold_sublanes(parts, row))
@@ -163,25 +163,47 @@
     out_ref[...] = wide[...].astype(BF16)
 
 
-def bundle_kernel(coupling_ref, bundle_a, bundle_b):
+def bundle_kernel(coupling_hbm, bundle_a_hbm, bundle_b_hbm, whole, bundle_a, bundle_b, sems):
+    fetch, put_a, put_b = [
+        [pltpu.make_async_copy(src.at[p], dst.at[p], sems.at[k, p]) for p in range(SEGMENT)]
+        for k, (src, dst) in enumerate(
+            ((coupling_hbm, whole), (bundle_a, bundle_a_hbm), (bundle_b, bundle_b_hbm))
+        )
+    ]
+    for copy in fetch:
+        copy.start()
     on_left = left(FEATURES)
-
-    @pl.loop(0, coupling_ref.shape[2], unroll=4)
-    def _(i):
-        low = coupling_ref[0, 0, i]
-        high = swap(coupling_ref[0, 1, i].astype(F32)).astype(BF16)
-        bundle_a[0, i] = jnp.where(on_left, low, high)
-        bundle_b[0, i] = jnp.where(on_left, high, low)
-
-
-def advance(side, coupling_ref, forcing_ref, first, state, record=None):
+    for p in range(SEGMENT):
+        fetch[p].wait()
+
+        @pl.loop(0, HALF // 8)
+        def _(block):
+            for k in range(8):
+                low = whole[p, block * 16 + k]
+                high = whole[p, block * 16 + 8 + k].astype(F32)
+                high = jnp.concatenate(
+                    [swap(high[j * 8 : j * 8 + 8]) for i in range(HALF // 8) for j in (2 * i + 1, 2 * i)],
+                    axis=0,
+                ).astype(BF16)
+                bundle_a[p, block * 8 + k] = jnp.where(on_left, low, high)
+                bundle_b[p, block * 8 + k] = jnp.where(on_left, high, low)
+
+        put_a[p].start()
+        put_b[p].start()
+    for copy in put_a + put_b:
+        copy.wait()
+
+
+def blocks8(x, odd):
+    return jnp.concatenate([x[j * 8 : j * 8 + 8] for j in range(odd, FEATURES // 8, 2)], axis=0)
+
+
+def advance(coupling_ref, forcing_ref, first, state, record=None):
     row = sublane_ids()
-    on_left = left(HALF)
 
     def step(position, state):
-        moved = swap(state)
-        both = [jnp.where(on_left, state, moved), jnp.where(on_left, moved, state)]
-        both = jnp.concatenate(both[::-1] if side else both, axis=0)
+        own = [state[j : j + 8] for j in range(0, HALF, 8)]
+        both = jnp.concatenate([x for block in own for x in (block, swap(block))], axis=0)
         state = forcing_ref[position] + matvec(coupling_ref, position, both, row)
         if record is not None:
             record[position] = state
@@ -225,11 +247,11 @@
     for p in range(SEGMENT):
         copies[p].wait()
         forcing = matvec(inverses_ref, p, lines[p], row)
-        low, high = forcing[:HALF], swap(forcing[HALF:])
+        low, high = blocks8(forcing, 0), swap(blocks8(forcing, 1))
         forcing_a[p] = jnp.where(on_left, low, high)
         forcing_b[p] = jnp.where(on_left, high, low)
     end_ref[...] = advance(
-        0, bundle_ref, forcing_a, lambda p: bundle_copies[p].wait(), forcing_a[0]
+        bundle_ref, forcing_a, lambda p: bundle_copies[p].wait(), forcing_a[0]
     )
     bundle_copies[0].wait()
 
@@ -245,22 +267,22 @@
     ]
     for copy in copies[1:] + copies[:1]:
         copy.start()
-    end_ref[...] = advance(1, bundle_ref, forcing_ref, lambda p: copies[p].wait(), forcing_ref[0])
+    end_ref[...] = advance(bundle_ref, forcing_ref, lambda p: copies[p].wait(), forcing_ref[0])
     copies[0].wait()
 
 
-def hop_kernel(hop, side, state_ref, coupling_ref, forcing_ref, end_ref):
+def hop_kernel(hop, state_ref, coupling_ref, forcing_ref, end_ref):
     @pl.when(here(hop))
     def _():
-        end_ref[...] = advance(side, coupling_ref, forcing_ref, 0, state_ref[...])
-
-
-def final_kernel(side, *refs):
+        end_ref[...] = advance(coupling_ref, forcing_ref, 0, state_ref[...])
+
+
+def final_kernel(*refs):
     *state_refs, coupling_ref, forcing_ref, solved_ref = refs
     state = state_refs[0][...]
     for ref in state_refs[1:]:
         state = state + ref[...]
-    advance(side, coupling_ref, forcing_ref, 0, state, solved_ref)
+    advance(coupling_ref, forcing_ref, 0, state, solved_ref)
 
 
 def return_pack_kernel(solved_a, solved_b, even_ref, odd_ref, out_ref):
@@ -273,7 +295,8 @@
         a, b = solved_a[position], solved_b[position]
         low = jnp.where(on_left, a, b)
         high = swap(jnp.where(on_left, b, a))
-        cells.append(jnp.concatenate([low, high], axis=0))
+        blocks = [x[j : j + 8] for j in range(0, HALF, 8) for x in (low, high)]
+        cells.append(jnp.concatenate(blocks, axis=0))
     rest = jnp.concatenate(cells, axis=1)
     high = rest.astype(BF16)
     low = (rest - high.astype(F32)).astype(BF16)
@@ -326,19 +349,21 @@
         name="pack_rows",
     )(hbm(elem_rows), send)
     arrived = exchange(outgoing)
-    split = 2
     bundles = pl.pallas_call(
         bundle_kernel,
         out_shape=[pltpu.HBM(bundle_shape.shape, BF16)] * 2,
-        grid=(SEGMENT, split),
-        in_specs=[
-            pl.BlockSpec((1, 2, HALF // split, FEATURES, LANES), lambda p, k: (p, 0, k, 0, 0))
+        in_specs=[in_hbm],
+        out_specs=[in_hbm] * 2,
+        scratch_shapes=[
+            pltpu.VMEM(coupling.shape, BF16),
+            pltpu.VMEM(bundle_shape.shape, BF16),
+            pltpu.VMEM(bundle_shape.shape, BF16),
+            pltpu.SemaphoreType.DMA((3, SEGMENT)),
         ],
-        out_specs=[pl.BlockSpec((1, HALF // split, FEATURES, LANES), lambda p, k: (p, k, 0, 0))] * 2,
-        compiler_params=params(16),
+        compiler_params=params(32),
         cost_estimate=pl.CostEstimate(flops=0, bytes_accessed=4 * coupling.size, transcendentals=0),
         name="bundle",
-    )(hbm(coupling.reshape(SEGMENT, 2, HALF, FEATURES, LANES)))
+    )(hbm(coupling))
     *forcings, even, odd, bundle_a, end_a = pl.pallas_call(
         forcing_kernel,
         out_shape=[forcing_shape] * 2 + [hot_shape] * 2 + [bundle_shape, state_shape],
@@ -386,12 +411,12 @@
         for side in range(2):
             end = (end_a, end_b)[side]
             if hop:
-                kernel = functools.partial(hop_kernel, hop, side)
+                kernel = functools.partial(hop_kernel, hop)
                 end = sweep(side, kernel, arrivals[side][-1:], state_shape, "hop_")
             pair = (hop % N_CIRC, (hop + 1) % N_CIRC)
             arrivals[side].append(lax.ppermute(end, "circ", [pair]))
     solved = [
-        sweep(side, functools.partial(final_kernel, side), arrivals[side][N_CIRC - 1 :], forcing_shape, "final_")
+        sweep(side, final_kernel, arrivals[side][N_CIRC - 1 :], forcing_shape, "final_")
         for side in range(2)
     ]
 

time: 156 us -> 146 us (0.936)
  Pallas kernels: 36.7 us -> 29.8 us
  blocking collectives: 55.4 us -> 52.4 us
  starting transfers between devices: 37.1 us -> 35.4 us
    pallas_call x1, Pallas kernels: 13.3 us -> 7.79 us  [local(): pl.pallas_call(bundle_kernel, out_shape=[pltpu.HBM(bundle_shape.shape, BF...]
    all_to_all x1, waiting for transfers between devices: 0.01 us -> 3.04 us  [exchange(): lax.all_to_all(blocks, ('circ', 'span'), split_axis=0, concat_axis=0, til...]
    all_to_all x1, blocking collectives: 55.4 us -> 52.4 us  [exchange(): lax.all_to_all(blocks, ('circ', 'span'), split_axis=0, concat_axis=0, til...]
    ppermute x30, starting transfers between devices: 25.6 us -> 23.9 us  [local(): arrivals[side].append(lax.ppermute(end, 'circ', [pair]))]
  transfers between devices with their start and end apart: 31 -> 31, of which waited for: 3 -> 5; matrix products, arithmetic and copies ran while one was open for 0% -> 0% of each run, Pallas kernels for 12% -> 8%
where the time goes in v3:
time: 146 us; the launch traced here: 145 us
  blocking collectives  52.4 us (36%)
  starting transfers between devices  35.4 us (24%)
  Pallas kernels  29.8 us (20%)
  waiting for transfers between devices  26.1 us (18%)
    all_to_all x1, blocking collectives, exchange(): lax.all_to_all(blocks, ('circ', 'span'), split_axis=0, concat_axis=0, til...  52.4 us
    ppermute x30, starting transfers between devices, local(): arrivals[side].append(lax.ppermute(end, 'circ', [pair]))  23.9 us
    ppermute x30, waiting for transfers between devices, local(): arrivals[side].append(lax.ppermute(end, 'circ', [pair]))  23.1 us
    all_to_all x1, starting transfers between devices, exchange(): lax.all_to_all(blocks, ('circ', 'span'), split_axis=0, concat_axis=0, til...  11.5 us
    pallas_call x1, Pallas kernels, local(): pl.pallas_call(bundle_kernel, out_shape=[pltpu.HBM(bundle_shape.shape, BF...  7.79 us
    pallas_call x1, Pallas kernels, local(): pl.pallas_call(forcing_kernel, out_shape=[forcing_shape] * 2 + [hot_shape...  7.5 us
    pallas_call x30, Pallas kernels, sweep(): pl.pallas_call(kernel, out_shape=shape, in_specs=[IN_VMEM] * len(operands...  5.54 us
    all_to_all x1, waiting for transfers between devices, exchange(): lax.all_to_all(blocks, ('circ', 'span'), split_axis=0, concat_axis=0, til...  3.04 us
  transfers between devices with their start and end apart: 31, of which 5 were waited for; matrix products, arithmetic and copies ran while one was open for 0% of the time, Pallas kernels for 8%

profile of v3, /device:TPU:1, one launch (start us, length us, event | category | flops | bytes accessed | tf_op | source)
XLA Modules:
  0.0 145.2 jit_solution(2508897151369054690)
XLA Ops:
  0.0 0.7 copy-done
  0.7 2.5 %pack_rows.1 = bf16[1024,128]{1,0:T(8,128)(2,1)} custom-call(bf16[80,768]{1,0:T(8,128)(2,1)} %rows_hbm.1, s32[12,1,128]{2,1,0:T(1,128)S(1)} %bitcast.9), custom_call_target="tpu_custom_call" | custom-call | tf_op jit(solution)/shard_map/pack_rows/pallas_call | solution.py:338
  3.2 11.5 %all-to-all-start = ((bf16[128,8,128]{2,1,0:T(8,128)(2,1)}), bf16[128,8,128]{2,1,0:T(8,128)(2,1)S(1)}, u32[]{:S(2)}, u32[]{:S(2)}) async-start(bf16[128,8,128]{2,1,0:T(8,128)(2,1)} %bitcast.1), calls=%async_computation | async-start | bytes 524288 | tf_op jit(solution)/shard_map/all_to_all | solution.py:325
  14.7 7.8 %bundle.1 = (bf16[6,40,80,128]{3,2,1,0:T(8,128)(2,1)}, bf16[6,40,80,128]{3,2,1,0:T(8,128)(2,1)}) custom-call(bf16[6,80,80,128]{3,2,1,0:T(8,128)(2,1)} %coupling_hbm.1), custom_call_target="tpu_custom_call" | custom-call | bytes 19660800 | tf_op jit(solution)/shard_map/bundle/pallas_call | solution.py:352
  22.5 3.0 %all-to-all-done = bf16[128,8,128]{2,1,0:T(8,128)(2,1)S(1)} async-done(((bf16[128,8,128]{2,1,0:T(8,128)(2,1)}), bf16[128,8,128]{2,1,0:T(8,128)(2,1)S(1)}, u32[]{:S(2)}, u32[]{:S(2)}) %all-to-all-start) | async-done | bytes 262176 | tf_op jit(solution)/shard_map/all_to_all | solution.py:325
  25.6 7.5 %forcing.1 = (f32[6,40,128]{2,1,0:T(8,128)S(1)}, f32[6,40,128]{2,1,0:T(8,128)S(1)}, bf16[768,768]{1,0:T(8,128)(2,1)S(1)}, bf16[768,768]{1,0:T(8,128)(2,1)S(1)}, ...) custom-call(bf16[1024,128]{1,0:T(8,128)(2,1)S(1)} %bitcast.8, s32[12,1,128]{2,1,0:T(1,128)S(1)} %bitcast.11, ...), custom_call_target="tpu_custom_call" | custom-call | tf_op jit(solution)/shard_map/forcing/pallas_call | solution.py:367
  33.1 2.4 %first_hop.1 = (f32[40,128]{1,0:T(8,128)S(1)}, bf16[6,40,80,128]{3,2,1,0:T(8,128)(2,1)S(1)}) custom-call(bf16[6,40,80,128]{3,2,1,0:T(8,128)(2,1)} %get-tuple-element.19.bundle_hbm, f32[6,40,128]{2,1,0:T(8,128)S(1)} %get-tuple-element.20.forcing_ref.refs_9_), custom_call_target="tpu_custom_call" | custom-call | tf_op jit(solution)/shard_map/first_hop/pallas_call | solution.py:384
  35.5 1.5 %collective-permute-start.15 = (f32[40,128]{1,0:T(8,128)S(1)}, f32[40,128]{1,0:T(8,128)S(1)}, u32[]{:S(2)}, u32[]{:S(2)}) collective-permute-start(f32[40,128]{1,0:T(8,128)S(1)} %get-tuple-element.21), channel_id=1, source_target_pairs={{0,16},{1,17},{2,18},{3,19},{4,20},{5,21},{6,22},{7,23},{8,24},{9,... | collective-permute-start | bytes 61448 | tf_op jit(solution)/shard_map/ppermute | solution.py:417
  37.1 1.3 collective-permute-start
  38.4 0.7 collective-permute-start.16
  39.1 0.2 collective-permute-done.state_ref
  39.3 0.7 collective-permute-start.1
  40.0 0.7 collective-permute-start.17
  40.7 0.7 collective-permute-start.2
  41.4 0.7 collective-permute-start.18
  42.1 0.7 collective-permute-start.3
  42.8 0.7 collective-permute-start.19
  43.5 0.7 collective-permute-start.4
  44.2 0.7 collective-permute-start.20
  44.9 0.7 collective-permute-start.5
  45.6 0.7 collective-permute-start.21
  46.3 0.7 collective-permute-start.6
  47.0 0.2 hop_b.20
  47.2 1.3 collective-permute-start.22
  48.5 1.3 collective-permute-start.7
  49.8 22.1 %collective-permute-done.22.state_ref.refs_0_ = f32[40,128]{1,0:T(8,128)S(1)} collective-permute-done((f32[40,128]{1,0:T(8,128)S(1)}, f32[40,128]{1,0:T(8,128)S(1)}, u32[]{:S(2)}, u32[]{:S(2)}) %collective-permute-start.22) | collective-permute-done | bytes 20512 | tf_op jit(solution)/shard_map/ppermute | solution.py:417
  72.0 1.2 hop_b.21
  73.2 1.3 collective-permute-start.23
  74.5 0.5 collective-permute-done.7.state_ref.refs_0_
  75.0 1.2 hop_a.21
  76.3 1.3 collective-permute-start.8
  77.6 0.7 collective-permute-start.24
  78.5 0.7 collective-permute-start.9
  79.2 0.7 collective-permute-start.25
  79.9 0.7 collective-permute-start.10
  80.6 0.7 collective-permute-start.26
  81.3 0.7 collective-permute-start.11
  82.0 0.7 collective-permute-start.27
  82.7 0.7 collective-permute-start.12
  83.4 0.7 collective-permute-start.28
  84.1 0.7 collective-permute-start.13
  84.8 0.7 collective-permute-start.29
  85.5 0.7 collective-permute-start.14
  86.2 1.2 final_b.1.solved_b
  87.5 1.2 final_a.1.solved_a
  88.7 1.5 %return_pack.1 = f32[1024,128]{1,0:T(8,128)S(1)} custom-call(f32[6,40,128]{2,1,0:T(8,128)S(1)} %final_a.1.solved_a, f32[6,40,128]{2,1,0:T(8,128)S(1)} %final_b.1.solved_b, bf16[768,768]{1,0:T(8,128)(2,1)S(1)} %get-tuple-element.23.even_ref, bf16[768,768]{1,0:T(8,128)(2,1)S(1)} %get-tuple-element.24.odd_ref), custom_call_target="tpu_custom_call" | custom-call | tf_op jit(solution)/shard_map/return_pack/pallas_call | solution.py:423
  90.3 52.4 %all_to_all.10 = f32[128,8,128]{2,1,0:T(8,128)S(1)} all-to-all(f32[128,8,128]{2,1,0:T(8,128)S(1)} %bitcast.7), channel_id=1, replica_groups=mesh['circ'=8,'span'=16] {'circ','span'}, dimensions={0} | all-to-all | bytes 1048576 | tf_op jit(solution)/shard_map/all_to_all | solution.py:325
  142.7 2.5 %return_rows.1 = f32[80,768]{1,0:T(8,128)} custom-call(f32[1024,128]{1,0:T(8,128)S(1)} %bitcast.6, s32[12,1,128]{2,1,0:T(1,128)S(1)} %bitcast.10), custom_call_target="tpu_custom_call" | custom-call | tf_op jit(solution)/shard_map/return_rows/pallas_call | solution.py:432
  (59 shorter events, 0.7 us)
Async XLA Ops:
  0.0 0.7 copy-start
  3.2 22.4 %all-to-all-start = ((bf16[128,8,128]{2,1,0:T(8,128)(2,1)}), bf16[128,8,128]{2,1,0:T(8,128)(2,1)S(1)}, u32[]{:S(2)}, u32[]{:S(2)}) async-start(bf16[128,8,128]{2,1,0:T(8,128)(2,1)} %bitcast.1), calls=%async_computation | async-start | bytes 524288 | tf_op jit(solution)/shard_map/all_to_all | solution.py:325
  14.7 10.9 %copy-start.2 = (s32[1,128,12]{1,0,2:T(1,128)S(1)}, s32[1,128,12]{1,0,2:T(1,128)}, u32[]{:S(2)}) copy-start(s32[1,128,12]{1,0,2:T(1,128)} %param.10) | copy-start | bytes 18436
  14.7 10.8 %copy-start.3 = (s32[1,128]{1,0:T(1,128)S(1)}, s32[1,128]{1,0:T(1,128)}, u32[]{:S(2)}) copy-start(s32[1,128]{1,0:T(1,128)} %counts_ref.1) | copy-start | bytes 1540
  35.5 2.9 %collective-permute-start.15 = (f32[40,128]{1,0:T(8,128)S(1)}, f32[40,128]{1,0:T(8,128)S(1)}, u32[]{:S(2)}, u32[]{:S(2)}) collective-permute-start(f32[40,128]{1,0:T(8,128)S(1)} %get-tuple-element.21), channel_id=1, source_target_pairs={{0,16},{1,17},{2,18},{3,19},{4,20},{5,21},{6,22},{7,23},{8,24},{9,... | collective-permute-start | bytes 61448 | tf_op jit(solution)/shard_map/ppermute | solution.py:417
  37.1 2.2 %collective-permute-start = (f32[40,128]{1,0:T(8,128)S(1)}, f32[40,128]{1,0:T(8,128)S(1)}, u32[]{:S(2)}, u32[]{:S(2)}) collective-permute-start(f32[40,128]{1,0:T(8,128)S(1)} %get-tuple-element.16), channel_id=1, source_target_pairs={{0,16},{1,17},{2,18},{3,19},{4,20},{5,21},{6,22},{7,23},{8,24},{9,... | collective-permute-start | bytes 61448 | tf_op jit(solution)/shard_map/ppermute | solution.py:417
  38.4 1.5 %collective-permute-start.16 = (f32[40,128]{1,0:T(8,128)S(1)}, f32[40,128]{1,0:T(8,128)S(1)}, u32[]{:S(2)}, u32[]{:S(2)}) collective-permute-start(f32[40,128]{1,0:T(8,128)S(1)} %hop_b.14), channel_id=1, source_target_pairs={{16,32},{17,33},{18,34},{19,35},{20,36},{21,37},{22,38},{23,39},{2... | collective-permute-start | bytes 61448 | tf_op jit(solution)/shard_map/ppermute | solution.py:417
  39.3 1.4 collective-permute-start.1
  40.0 1.4 collective-permute-start.17
  40.7 1.4 collective-permute-start.2
  41.4 1.4 collective-permute-start.18
  42.1 1.4 collective-permute-start.3
  42.8 1.4 collective-permute-start.19
  43.5 1.4 collective-permute-start.4
  44.2 1.4 collective-permute-start.20
  44.9 1.4 collective-permute-start.5
  45.6 1.4 collective-permute-start.21
  46.3 2.2 %collective-permute-start.6 = (f32[40,128]{1,0:T(8,128)S(1)}, f32[40,128]{1,0:T(8,128)S(1)}, u32[]{:S(2)}, u32[]{:S(2)}) collective-permute-start(f32[40,128]{1,0:T(8,128)S(1)} %hop_a.19), channel_id=1, source_target_pairs={{96,112},{97,113},{98,114},{99,115},{100,116},{101,117},{102,118},... | collective-permute-start | bytes 61448 | tf_op jit(solution)/shard_map/ppermute | solution.py:417
  47.2 24.8 %collective-permute-start.22 = (f32[40,128]{1,0:T(8,128)S(1)}, f32[40,128]{1,0:T(8,128)S(1)}, u32[]{:S(2)}, u32[]{:S(2)}) collective-permute-start(f32[40,128]{1,0:T(8,128)S(1)} %hop_b.20), channel_id=1, source_target_pairs={{112,0},{113,1},{114,2},{115,3},{116,4},{117,5},{118,6},{119,7},{1... | collective-permute-start | bytes 61448 | tf_op jit(solution)/shard_map/ppermute | solution.py:417
  48.5 26.5 %collective-permute-start.7 = (f32[40,128]{1,0:T(8,128)S(1)}, f32[40,128]{1,0:T(8,128)S(1)}, u32[]{:S(2)}, u32[]{:S(2)}) collective-permute-start(f32[40,128]{1,0:T(8,128)S(1)} %hop_a.20), channel_id=1, source_target_pairs={{112,0},{113,1},{114,2},{115,3},{116,4},{117,5},{118,6},{119,7},{1... | collective-permute-start | bytes 61448 | tf_op jit(solution)/shard_map/ppermute | solution.py:417
  73.2 4.4 %collective-permute-start.23 = (f32[40,128]{1,0:T(8,128)S(1)}, f32[40,128]{1,0:T(8,128)S(1)}, u32[]{:S(2)}, u32[]{:S(2)}) collective-permute-start(f32[40,128]{1,0:T(8,128)S(1)} %hop_b.21), channel_id=1, source_target_pairs={{0,16},{1,17},{2,18},{3,19},{4,20},{5,21},{6,22},{7,23},{8,24},{9,... | collective-permute-start | bytes 61448 | tf_op jit(solution)/shard_map/ppermute | solution.py:417
  76.3 2.2 %collective-permute-start.8 = (f32[40,128]{1,0:T(8,128)S(1)}, f32[40,128]{1,0:T(8,128)S(1)}, u32[]{:S(2)}, u32[]{:S(2)}) collective-permute-start(f32[40,128]{1,0:T(8,128)S(1)} %hop_a.21), channel_id=1, source_target_pairs={{0,16},{1,17},{2,18},{3,19},{4,20},{5,21},{6,22},{7,23},{8,24},{9,... | collective-permute-start | bytes 61448 | tf_op jit(solution)/shard_map/ppermute | solution.py:417
  77.6 1.5 %collective-permute-start.24 = (f32[40,128]{1,0:T(8,128)S(1)}, f32[40,128]{1,0:T(8,128)S(1)}, u32[]{:S(2)}, u32[]{:S(2)}) collective-permute-start(f32[40,128]{1,0:T(8,128)S(1)} %hop_b.22), channel_id=1, source_target_pairs={{16,32},{17,33},{18,34},{19,35},{20,36},{21,37},{22,38},{23,39},{2... | collective-permute-start | bytes 61448 | tf_op jit(solution)/shard_map/ppermute | solution.py:417
  78.5 1.4 collective-permute-start.9
  79.2 1.4 collective-permute-start.25
  79.9 1.4 collective-permute-start.10
  80.6 1.4 collective-permute-start.26
  81.3 1.4 collective-permute-start.11
  82.0 1.4 collective-permute-start.27
  82.7 1.4 collective-permute-start.12
  83.4 1.4 collective-permute-start.28
  84.1 1.4 collective-permute-start.13
  84.8 1.4 collective-permute-start.29
  85.5 1.9 %collective-permute-start.14 = (f32[40,128]{1,0:T(8,128)S(1)}, f32[40,128]{1,0:T(8,128)S(1)}, u32[]{:S(2)}, u32[]{:S(2)}) collective-permute-start(f32[40,128]{1,0:T(8,128)S(1)} %hop_a.27), channel_id=1, source_target_pairs={{96,112},{97,113},{98,114},{99,115},{100,116},{101,117},{102,118},... | collective-permute-start | bytes 61448 | tf_op jit(solution)/shard_map/ppermute | solution.py:417
  87.4 55.3 %copy-start.1 = (s32[1,128,12]{1,0,2:T(1,128)S(1)}, s32[1,128,12]{1,0,2:T(1,128)}, u32[]{:S(2)}) copy-start(s32[1,128,12]{1,0,2:T(1,128)} %param.9) | copy-start | bytes 18436

commit v4 on v3

--- a/solution.py
+++ b/solution.py
@@ -210,11 +210,13 @@
         return state
 
     if callable(first):
-        for position in range(1, SEGMENT):
+
+        def waited(position, state):
             first(position)
-            state = step(position, state)
-        return state
-    return lax.fori_loop(first, SEGMENT, step, state)
+            return step(position, state)
+
+        return lax.fori_loop(1, SEGMENT, waited, state)
+    return lax.fori_loop(first, SEGMENT, step, state, unroll=True)
 
 
 def forcing_kernel(
@@ -222,18 +224,16 @@
     forcing_a, forcing_b, even_ref, odd_ref, bundle_ref, end_ref,
     wide, lines, inverses_ref, sems, bundle_sems,
 ):
-    copies = [
-        pltpu.make_async_copy(inverses_hbm.at[p], inverses_ref.at[p], sems.at[p])
-        for p in range(SEGMENT)
-    ]
-    for copy in copies:
-        copy.start()
-    bundle_copies = [
-        pltpu.make_async_copy(bundle_hbm.at[p], bundle_ref.at[p], bundle_sems.at[p])
-        for p in range(SEGMENT)
-    ]
-    for copy in bundle_copies[1:] + bundle_copies[:1]:
-        copy.start()
+    def copy(p):
+        return pltpu.make_async_copy(inverses_hbm.at[p], inverses_ref.at[p], sems.at[p])
+
+    def bundle_copy(p):
+        return pltpu.make_async_copy(bundle_hbm.at[p], bundle_ref.at[p], bundle_sems.at[p])
+
+    for p in range(SEGMENT):
+        copy(p).start()
+    for p in range(1, SEGMENT):
+        bundle_copy(p).start()
     wide[...] = arrived_ref[...].astype(F32)
     slot = lax.broadcasted_iota(jnp.int32, (SLOTS, PEERS), 0)
     index = columns(jnp.where(slot < counts_ref[...], cells_ref[...].reshape(SLOTS, PEERS), -1))
@@ -244,16 +244,17 @@
         lines[p] = found[:, p * LINES : (p + 1) * LINES]
     row = sublane_ids()
     on_left = left(HALF)
-    for p in range(SEGMENT):
-        copies[p].wait()
+
+    @pl.loop(0, SEGMENT)
+    def _(p):
+        copy(p).wait()
         forcing = matvec(inverses_ref, p, lines[p], row)
         low, high = blocks8(forcing, 0), swap(blocks8(forcing, 1))
         forcing_a[p] = jnp.where(on_left, low, high)
         forcing_b[p] = jnp.where(on_left, high, low)
     end_ref[...] = advance(
-        bundle_ref, forcing_a, lambda p: bundle_copies[p].wait(), forcing_a[0]
+        bundle_ref, forcing_a, lambda p: bundle_copy(p).wait(), forcing_a[0]
     )
-    bundle_copies[0].wait()
 
 
 def here(hop):
@@ -261,14 +262,29 @@
 
 
 def first_hop_kernel(bundle_hbm, forcing_ref, end_ref, bundle_ref, sems):
-    copies = [
-        pltpu.make_async_copy(bundle_hbm.at[p], bundle_ref.at[p], sems.at[p])
-        for p in range(SEGMENT)
-    ]
-    for copy in copies[1:] + copies[:1]:
-        copy.start()
-    end_ref[...] = advance(bundle_ref, forcing_ref, lambda p: copies[p].wait(), forcing_ref[0])
-    copies[0].wait()
+    def copy(p):
+        return pltpu.make_async_copy(bundle_hbm.at[p], bundle_ref.at[p], sems.at[p])
+
+    for p in range(1, SEGMENT):
+        copy(p).start()
+    end_ref[...] = advance(bundle_ref, forcing_ref, lambda p: copy(p).wait(), forcing_ref[0])
+
+
+def widen_kernel(bundle_hbm, bundle_ref, wide_ref, first, sem):
+    copy = pltpu.make_async_copy(bundle_hbm.at[0], first, sem)
+    copy.start()
+
+    @pl.loop(1, SEGMENT)
+    def _(p):
+        @pl.loop(0, HALF, unroll=8)
+        def _(i):
+            wide_ref[p, i] = bundle_ref[p, i].astype(F32)
+
+    copy.wait()
+
+    @pl.loop(0, HALF, unroll=8)
+    def _(i):
+        wide_ref[0, i] = first[i].astype(F32)
 
 
 def hop_kernel(hop, state_ref, coupling_ref, forcing_ref, end_ref):
@@ -390,7 +406,26 @@
         compiler_params=params(8),
         name="first_hop",
     )(hbm(bundles[1]), forcings[1])
-    bundles = [vmem(bundle_a), vmem(bundle_b)]
+    bundles = [
+        vmem(
+            pl.pallas_call(
+                widen_kernel,
+                out_shape=jax.ShapeDtypeStruct(bundle_shape.shape, F32),
+                in_specs=[in_hbm, IN_VMEM],
+                out_specs=IN_VMEM,
+                scratch_shapes=[
+                    pltpu.VMEM(bundle_shape.shape[1:], BF16),
+                    pltpu.SemaphoreType.DMA,
+                ],
+                compiler_params=params(4),
+                cost_estimate=pl.CostEstimate(
+                    flops=2 * 10**6, bytes_accessed=2 * bundle_shape.size, transcendentals=0
+                ),
+                name="widen",
+            )(hbm(source), vmem(near))
+        )
+        for source, near in zip(bundles, (bundle_a, bundle_b))
+    ]
 
     def sweep(side, kernel, states, shape, name):
         operands = [*states, bundles[side], forcings[side]]

time: 146 us -> 139 us (0.952)
  waiting for transfers between devices: 26.1 us -> 21.2 us
  blocking collectives: 52.4 us -> 49.2 us
    ppermute x30, waiting for transfers between devices: 23.1 us -> 18.2 us  [local(): arrivals[side].append(lax.ppermute(end, 'circ', [pair]))]
    all_to_all x1, blocking collectives: 52.4 us -> 49.2 us  [exchange(): lax.all_to_all(blocks, ('circ', 'span'), split_axis=0, concat_axis=0, til...]
    pallas_call x0 -> x2, Pallas kernels: none -> 2.54 us  [local(): pl.pallas_call(widen_kernel, out_shape=jax.ShapeDtypeStruct(bundle_shape....]
  transfers between devices with their start and end apart: 31 -> 31, of which waited for: 5 -> 4; matrix products, arithmetic and copies ran while one was open for 0% -> 0% of each run, Pallas kernels for 8% -> 12%
where the time goes in v4:
time: 139 us; the launch traced here: 138 us
  blocking collectives  49.2 us (35%)
  starting transfers between devices  35.4 us (25%)
  Pallas kernels  30.9 us (22%)
  waiting for transfers between devices  21.2 us (15%)
    all_to_all x1, blocking collectives, exchange(): lax.all_to_all(blocks, ('circ', 'span'), split_axis=0, concat_axis=0, til...  49.2 us
    ppermute x30, starting transfers between devices, local(): arrivals[side].append(lax.ppermute(end, 'circ', [pair]))  23.9 us
    ppermute x30, waiting for transfers between devices, local(): arrivals[side].append(lax.ppermute(end, 'circ', [pair]))  18.2 us
    all_to_all x1, starting transfers between devices, exchange(): lax.all_to_all(blocks, ('circ', 'span'), split_axis=0, concat_axis=0, til...  11.5 us
    pallas_call x1, Pallas kernels, local(): pl.pallas_call(bundle_kernel, out_shape=[pltpu.HBM(bundle_shape.shape, BF...  7.79 us
    pallas_call x1, Pallas kernels, local(): pl.pallas_call(forcing_kernel, out_shape=[forcing_shape] * 2 + [hot_shape...  7.45 us
    pallas_call x30, Pallas kernels, sweep(): pl.pallas_call(kernel, out_shape=shape, in_specs=[IN_VMEM] * len(operands...  4.17 us
    all_to_all x1, waiting for transfers between devices, exchange(): lax.all_to_all(blocks, ('circ', 'span'), split_axis=0, concat_axis=0, til...  3.04 us
  transfers between devices with their start and end apart: 31, of which 4 were waited for; matrix products, arithmetic and copies ran while one was open for 0% of the time, Pallas kernels for 12%

profile of v4, /device:TPU:1, one launch (start us, length us, event | category | flops | bytes accessed | tf_op | source)
XLA Modules:
  0.0 138.1 jit_solution(8358239628268225257)
XLA Ops:
  0.0 0.7 copy-done
  0.7 2.5 %pack_rows.1 = bf16[1024,128]{1,0:T(8,128)(2,1)} custom-call(bf16[80,768]{1,0:T(8,128)(2,1)} %rows_hbm.1, s32[12,1,128]{2,1,0:T(1,128)S(1)} %bitcast.9), custom_call_target="tpu_custom_call" | custom-call | tf_op jit(solution)/shard_map/pack_rows/pallas_call | solution.py:354
  3.2 11.5 %all-to-all-start = ((bf16[128,8,128]{2,1,0:T(8,128)(2,1)}), bf16[128,8,128]{2,1,0:T(8,128)(2,1)S(1)}, u32[]{:S(2)}, u32[]{:S(2)}) async-start(bf16[128,8,128]{2,1,0:T(8,128)(2,1)} %bitcast.1), calls=%async_computation | async-start | bytes 524288 | tf_op jit(solution)/shard_map/all_to_all | solution.py:341
  14.7 7.8 %bundle.1 = (bf16[6,40,80,128]{3,2,1,0:T(8,128)(2,1)}, bf16[6,40,80,128]{3,2,1,0:T(8,128)(2,1)}) custom-call(bf16[6,80,80,128]{3,2,1,0:T(8,128)(2,1)} %coupling_hbm.1), custom_call_target="tpu_custom_call" | custom-call | bytes 19660800 | tf_op jit(solution)/shard_map/bundle/pallas_call | solution.py:368
  22.5 3.0 %all-to-all-done = bf16[128,8,128]{2,1,0:T(8,128)(2,1)S(1)} async-done(((bf16[128,8,128]{2,1,0:T(8,128)(2,1)}), bf16[128,8,128]{2,1,0:T(8,128)(2,1)S(1)}, u32[]{:S(2)}, u32[]{:S(2)}) %all-to-all-start) | async-done | bytes 262176 | tf_op jit(solution)/shard_map/all_to_all | solution.py:341
  25.6 7.5 %forcing.1 = (f32[6,40,128]{2,1,0:T(8,128)S(1)}, f32[6,40,128]{2,1,0:T(8,128)S(1)}, bf16[768,768]{1,0:T(8,128)(2,1)S(1)}, bf16[768,768]{1,0:T(8,128)(2,1)S(1)}, ...) custom-call(bf16[1024,128]{1,0:T(8,128)(2,1)S(1)} %bitcast.8, s32[12,1,128]{2,1,0:T(1,128)S(1)} %bitcast.11, ...), custom_call_target="tpu_custom_call" | custom-call | tf_op jit(solution)/shard_map/forcing/pallas_call | solution.py:383
  33.0 1.5 %collective-permute-start = (f32[40,128]{1,0:T(8,128)S(1)}, f32[40,128]{1,0:T(8,128)S(1)}, u32[]{:S(2)}, u32[]{:S(2)}) collective-permute-start(f32[40,128]{1,0:T(8,128)S(1)} %get-tuple-element.16), channel_id=1, source_target_pairs={{0,16},{1,17},{2,18},{3,19},{4,20},{5,21},{6,22},{7,23},{8,24},{9,... | collective-permute-start | bytes 61448 | tf_op jit(solution)/shard_map/ppermute | solution.py:452
  34.6 2.4 %first_hop.1 = (f32[40,128]{1,0:T(8,128)S(1)}, bf16[6,40,80,128]{3,2,1,0:T(8,128)(2,1)S(1)}) custom-call(bf16[6,40,80,128]{3,2,1,0:T(8,128)(2,1)} %get-tuple-element.19.bundle_hbm, f32[6,40,128]{2,1,0:T(8,128)S(1)} %get-tuple-element.20.forcing_ref.refs_9_), custom_call_target="tpu_custom_call" | custom-call | tf_op jit(solution)/shard_map/first_hop/pallas_call | solution.py:400
  37.0 1.3 collective-permute-start.15
  38.3 1.3 widen.2.coupling_ref.refs_8_
  39.6 1.3 widen.3.coupling_ref.refs_8_
  40.9 0.7 collective-permute-start.1
  41.6 0.7 collective-permute-start.16
  42.3 0.7 collective-permute-start.2
  43.0 0.7 collective-permute-start.17
  43.7 0.7 collective-permute-start.3
  44.4 0.7 collective-permute-start.18
  45.1 0.7 collective-permute-start.4
  46.0 0.7 collective-permute-start.19
  46.7 0.7 collective-permute-start.5
  47.4 0.7 collective-permute-start.20
  48.1 0.7 collective-permute-start.6
  48.8 0.7 collective-permute-start.21
  49.5 1.3 collective-permute-start.7
  50.9 1.3 collective-permute-start.22
  52.2 17.6 %collective-permute-done.7.state_ref.refs_0_ = f32[40,128]{1,0:T(8,128)S(1)} collective-permute-done((f32[40,128]{1,0:T(8,128)S(1)}, f32[40,128]{1,0:T(8,128)S(1)}, u32[]{:S(2)}, u32[]{:S(2)}) %collective-permute-start.7) | collective-permute-done | bytes 20512 | tf_op jit(solution)/shard_map/ppermute | solution.py:452
  69.7 0.8 hop_a.21
  70.6 1.3 collective-permute-start.8
  71.9 0.3 collective-permute-done.22.state_ref.refs_0_
  72.2 0.8 hop_b.21
  73.0 1.3 collective-permute-start.23
  74.4 0.7 collective-permute-start.9
  75.2 0.7 collective-permute-start.24
  75.9 0.7 collective-permute-start.10
  76.6 0.7 collective-permute-start.25
  77.5 0.7 collective-permute-start.11
  78.3 0.7 collective-permute-start.26
  79.0 0.7 collective-permute-start.12
  79.7 0.7 collective-permute-start.27
  80.4 0.7 collective-permute-start.13
  81.1 0.7 collective-permute-start.28
  81.8 0.7 collective-permute-start.14
  82.5 0.7 collective-permute-start.29
  83.2 0.8 final_a.1.solved_a
  84.0 0.8 final_b.1.solved_b
  84.9 1.5 %return_pack.1 = f32[1024,128]{1,0:T(8,128)S(1)} custom-call(f32[6,40,128]{2,1,0:T(8,128)S(1)} %final_a.1.solved_a, f32[6,40,128]{2,1,0:T(8,128)S(1)} %final_b.1.solved_b, bf16[768,768]{1,0:T(8,128)(2,1)S(1)} %get-tuple-element.23.even_ref, bf16[768,768]{1,0:T(8,128)(2,1)S(1)} %get-tuple-element.24.odd_ref), custom_call_target="tpu_custom_call" | custom-call | tf_op jit(solution)/shard_map/return_pack/pallas_call | solution.py:458
  86.4 49.2 %all_to_all.10 = f32[128,8,128]{2,1,0:T(8,128)S(1)} all-to-all(f32[128,8,128]{2,1,0:T(8,128)S(1)} %bitcast.7), channel_id=1, replica_groups=mesh['circ'=8,'span'=16] {'circ','span'}, dimensions={0} | all-to-all | bytes 1048576 | tf_op jit(solution)/shard_map/all_to_all | solution.py:341
  135.6 2.5 %return_rows.1 = f32[80,768]{1,0:T(8,128)} custom-call(f32[1024,128]{1,0:T(8,128)S(1)} %bitcast.6, s32[12,1,128]{2,1,0:T(1,128)S(1)} %bitcast.10), custom_call_target="tpu_custom_call" | custom-call | tf_op jit(solution)/shard_map/return_rows/pallas_call | solution.py:467
  (61 shorter events, 1.1 us)
Async XLA Ops:
  0.0 0.7 copy-start
  3.2 22.4 %all-to-all-start = ((bf16[128,8,128]{2,1,0:T(8,128)(2,1)}), bf16[128,8,128]{2,1,0:T(8,128)(2,1)S(1)}, u32[]{:S(2)}, u32[]{:S(2)}) async-start(bf16[128,8,128]{2,1,0:T(8,128)(2,1)} %bitcast.1), calls=%async_computation | async-start | bytes 524288 | tf_op jit(solution)/shard_map/all_to_all | solution.py:341
  14.7 10.9 %copy-start.2 = (s32[1,128,12]{1,0,2:T(1,128)S(1)}, s32[1,128,12]{1,0,2:T(1,128)}, u32[]{:S(2)}) copy-start(s32[1,128,12]{1,0,2:T(1,128)} %param.10) | copy-start | bytes 18436
  14.7 10.8 %copy-start.3 = (s32[1,128]{1,0:T(1,128)S(1)}, s32[1,128]{1,0:T(1,128)}, u32[]{:S(2)}) copy-start(s32[1,128]{1,0:T(1,128)} %counts_ref.1) | copy-start | bytes 1540
  33.0 7.8 %collective-permute-start = (f32[40,128]{1,0:T(8,128)S(1)}, f32[40,128]{1,0:T(8,128)S(1)}, u32[]{:S(2)}, u32[]{:S(2)}) collective-permute-start(f32[40,128]{1,0:T(8,128)S(1)} %get-tuple-element.16), channel_id=1, source_target_pairs={{0,16},{1,17},{2,18},{3,19},{4,20},{5,21},{6,22},{7,23},{8,24},{9,... | collective-permute-start | bytes 61448 | tf_op jit(solution)/shard_map/ppermute | solution.py:452
  37.0 4.6 %collective-permute-start.15 = (f32[40,128]{1,0:T(8,128)S(1)}, f32[40,128]{1,0:T(8,128)S(1)}, u32[]{:S(2)}, u32[]{:S(2)}) collective-permute-start(f32[40,128]{1,0:T(8,128)S(1)} %get-tuple-element.21), channel_id=1, source_target_pairs={{0,16},{1,17},{2,18},{3,19},{4,20},{5,21},{6,22},{7,23},{8,24},{9,... | collective-permute-start | bytes 61448 | tf_op jit(solution)/shard_map/ppermute | solution.py:452
  40.9 1.4 collective-permute-start.1
  41.6 1.4 collective-permute-start.16
  42.3 1.4 collective-permute-start.2
  43.0 1.4 collective-permute-start.17
  43.7 1.4 collective-permute-start.3
  44.4 1.4 collective-permute-start.18
  45.1 1.6 %collective-permute-start.4 = (f32[40,128]{1,0:T(8,128)S(1)}, f32[40,128]{1,0:T(8,128)S(1)}, u32[]{:S(2)}, u32[]{:S(2)}) collective-permute-start(f32[40,128]{1,0:T(8,128)S(1)} %hop_a.17), channel_id=1, source_target_pairs={{64,80},{65,81},{66,82},{67,83},{68,84},{69,85},{70,86},{71,87},{7... | collective-permute-start | bytes 61448 | tf_op jit(solution)/shard_map/ppermute | solution.py:452
  46.0 1.4 collective-permute-start.19
  46.7 1.4 collective-permute-start.5
  47.4 1.4 collective-permute-start.20
  48.1 1.4 collective-permute-start.6
  48.8 2.0 %collective-permute-start.21 = (f32[40,128]{1,0:T(8,128)S(1)}, f32[40,128]{1,0:T(8,128)S(1)}, u32[]{:S(2)}, u32[]{:S(2)}) collective-permute-start(f32[40,128]{1,0:T(8,128)S(1)} %hop_b.19), channel_id=1, source_target_pairs={{96,112},{97,113},{98,114},{99,115},{100,116},{101,117},{102,118},... | collective-permute-start | bytes 61448 | tf_op jit(solution)/shard_map/ppermute | solution.py:452
  49.5 20.2 %collective-permute-start.7 = (f32[40,128]{1,0:T(8,128)S(1)}, f32[40,128]{1,0:T(8,128)S(1)}, u32[]{:S(2)}, u32[]{:S(2)}) collective-permute-start(f32[40,128]{1,0:T(8,128)S(1)} %hop_a.20), channel_id=1, source_target_pairs={{112,0},{113,1},{114,2},{115,3},{116,4},{117,5},{118,6},{119,7},{1... | collective-permute-start | bytes 61448 | tf_op jit(solution)/shard_map/ppermute | solution.py:452
  50.9 21.3 %collective-permute-start.22 = (f32[40,128]{1,0:T(8,128)S(1)}, f32[40,128]{1,0:T(8,128)S(1)}, u32[]{:S(2)}, u32[]{:S(2)}) collective-permute-start(f32[40,128]{1,0:T(8,128)S(1)} %hop_b.20), channel_id=1, source_target_pairs={{112,0},{113,1},{114,2},{115,3},{116,4},{117,5},{118,6},{119,7},{1... | collective-permute-start | bytes 61448 | tf_op jit(solution)/shard_map/ppermute | solution.py:452
  70.6 3.8 %collective-permute-start.8 = (f32[40,128]{1,0:T(8,128)S(1)}, f32[40,128]{1,0:T(8,128)S(1)}, u32[]{:S(2)}, u32[]{:S(2)}) collective-permute-start(f32[40,128]{1,0:T(8,128)S(1)} %hop_a.21), channel_id=1, source_target_pairs={{0,16},{1,17},{2,18},{3,19},{4,20},{5,21},{6,22},{7,23},{8,24},{9,... | collective-permute-start | bytes 61448 | tf_op jit(solution)/shard_map/ppermute | solution.py:452
  73.0 2.2 %collective-permute-start.23 = (f32[40,128]{1,0:T(8,128)S(1)}, f32[40,128]{1,0:T(8,128)S(1)}, u32[]{:S(2)}, u32[]{:S(2)}) collective-permute-start(f32[40,128]{1,0:T(8,128)S(1)} %hop_b.21), channel_id=1, source_target_pairs={{0,16},{1,17},{2,18},{3,19},{4,20},{5,21},{6,22},{7,23},{8,24},{9,... | collective-permute-start | bytes 61448 | tf_op jit(solution)/shard_map/ppermute | solution.py:452
  74.4 1.5 %collective-permute-start.9 = (f32[40,128]{1,0:T(8,128)S(1)}, f32[40,128]{1,0:T(8,128)S(1)}, u32[]{:S(2)}, u32[]{:S(2)}) collective-permute-start(f32[40,128]{1,0:T(8,128)S(1)} %hop_a.22), channel_id=1, source_target_pairs={{16,32},{17,33},{18,34},{19,35},{20,36},{21,37},{22,38},{23,39},{2... | collective-permute-start | bytes 61448 | tf_op jit(solution)/shard_map/ppermute | solution.py:452
  75.2 1.4 collective-permute-start.24
  75.9 1.4 collective-permute-start.10
  76.6 1.6 %collective-permute-start.25 = (f32[40,128]{1,0:T(8,128)S(1)}, f32[40,128]{1,0:T(8,128)S(1)}, u32[]{:S(2)}, u32[]{:S(2)}) collective-permute-start(f32[40,128]{1,0:T(8,128)S(1)} %hop_b.23), channel_id=1, source_target_pairs={{32,48},{33,49},{34,50},{35,51},{36,52},{37,53},{38,54},{39,55},{4... | collective-permute-start | bytes 61448 | tf_op jit(solution)/shard_map/ppermute | solution.py:452
  77.5 1.4 collective-permute-start.11
  78.3 1.4 collective-permute-start.26
  79.0 1.4 collective-permute-start.12
  79.7 1.4 collective-permute-start.27
  80.4 1.4 collective-permute-start.13
  81.1 1.4 collective-permute-start.28
  81.8 1.4 collective-permute-start.14
  82.5 1.5 %collective-permute-start.29 = (f32[40,128]{1,0:T(8,128)S(1)}, f32[40,128]{1,0:T(8,128)S(1)}, u32[]{:S(2)}, u32[]{:S(2)}) collective-permute-start(f32[40,128]{1,0:T(8,128)S(1)} %hop_b.27), channel_id=1, source_target_pairs={{96,112},{97,113},{98,114},{99,115},{100,116},{101,117},{102,118},... | collective-permute-start | bytes 61448 | tf_op jit(solution)/shard_map/ppermute | solution.py:452
  84.0 51.6 %copy-start.1 = (s32[1,128,12]{1,0,2:T(1,128)S(1)}, s32[1,128,12]{1,0,2:T(1,128)}, u32[]{:S(2)}) copy-start(s32[1,128,12]{1,0,2:T(1,128)} %param.9) | copy-start | bytes 18436

commit v5 on v4

--- a/solution.py
+++ b/solution.py
@@ -18,6 +18,7 @@
 MAIN = 64
 TAIL = FEATURES - MAIN
 N_CIRC = 8
+NEAR = 2
 HALF = FEATURES // 2
 LANES = 128
 SIDE = LANES // 2
@@ -163,7 +164,10 @@
     out_ref[...] = wide[...].astype(BF16)
 
 
-def bundle_kernel(coupling_hbm, bundle_a_hbm, bundle_b_hbm, whole, bundle_a, bundle_b, sems):
+def bundle_kernel(
+    coupling_hbm, inverses_hbm, bundle_a_hbm, bundle_b_hbm, near_ref,
+    whole, bundle_a, bundle_b, sems, near_sem,
+):
     fetch, put_a, put_b = [
         [pltpu.make_async_copy(src.at[p], dst.at[p], sems.at[k, p]) for p in range(SEGMENT)]
         for k, (src, dst) in enumerate(
@@ -172,6 +176,8 @@
     ]
     for copy in fetch:
         copy.start()
+    near = pltpu.make_async_copy(inverses_hbm.at[pl.ds(0, NEAR)], near_ref, near_sem)
+    near.start()
     on_left = left(FEATURES)
     for p in range(SEGMENT):
         fetch[p].wait()
@@ -192,6 +198,7 @@
         put_b[p].start()
     for copy in put_a + put_b:
         copy.wait()
+    near.wait()
 
 
 def blocks8(x, odd):
@@ -220,8 +227,8 @@
 
 
 def forcing_kernel(
-    arrived_ref, cells_ref, counts_ref, inverses_hbm, bundle_hbm,
-    forcing_a, forcing_b, even_ref, odd_ref, bundle_ref, end_ref,
+    arrived_ref, cells_ref, counts_ref, near_ref, inverses_hbm, bundle_hbm,
+    forcing_a, forcing_b, bundle_ref, end_ref,
     wide, lines, inverses_ref, sems, bundle_sems,
 ):
     def copy(p):
@@ -230,31 +237,49 @@
     def bundle_copy(p):
         return pltpu.make_async_copy(bundle_hbm.at[p], bundle_ref.at[p], bundle_sems.at[p])
 
-    for p in range(SEGMENT):
+    for p in range(NEAR, SEGMENT):
         copy(p).start()
-    for p in range(1, SEGMENT):
-        bundle_copy(p).start()
     wide[...] = arrived_ref[...].astype(F32)
     slot = lax.broadcasted_iota(jnp.int32, (SLOTS, PEERS), 0)
     index = columns(jnp.where(slot < counts_ref[...], cells_ref[...].reshape(SLOTS, PEERS), -1))
     hots = one_hot(index, 0), one_hot(index, 1)
-    even_ref[...], odd_ref[...] = hots
     found = unpack(lambda r: wide[pl.ds(r, PEERS, stride=ROWS), :], hots, 1)
     for p in range(SEGMENT):
         lines[p] = found[:, p * LINES : (p + 1) * LINES]
     row = sublane_ids()
     on_left = left(HALF)
 
-    @pl.loop(0, SEGMENT)
-    def _(p):
-        copy(p).wait()
-        forcing = matvec(inverses_ref, p, lines[p], row)
+    def force(p, blocks_ref):
+        forcing = matvec(blocks_ref, p, lines[p], row)
         low, high = blocks8(forcing, 0), swap(blocks8(forcing, 1))
         forcing_a[p] = jnp.where(on_left, low, high)
         forcing_b[p] = jnp.where(on_left, high, low)
+
+    @pl.loop(0, NEAR)
+    def _(p):
+        bundle_copy(p + 1).start()
+        force(p, near_ref)
+
+    @pl.loop(NEAR, SEGMENT)
+    def _(p):
+        copy(p).wait()
+
+        @pl.when(p + 1 < SEGMENT)
+        def _():
+            bundle_copy(p + 1).start()
+
+        force(p, inverses_ref)
+
     end_ref[...] = advance(
         bundle_ref, forcing_a, lambda p: bundle_copy(p).wait(), forcing_a[0]
     )
+
+
+def hots_kernel(cells_ref, counts_ref, even_ref, odd_ref):
+    slot = lax.broadcasted_iota(jnp.int32, (SLOTS, PEERS), 0)
+    index = columns(jnp.where(slot < counts_ref[...], cells_ref[...].reshape(SLOTS, PEERS), -1))
+    even_ref[...] = one_hot(index, 0)
+    odd_ref[...] = one_hot(index, 1)
 
 
 def here(hop):
@@ -365,26 +390,28 @@
         name="pack_rows",
     )(hbm(elem_rows), send)
     arrived = exchange(outgoing)
-    bundles = pl.pallas_call(
+    *bundles, near = pl.pallas_call(
         bundle_kernel,
-        out_shape=[pltpu.HBM(bundle_shape.shape, BF16)] * 2,
-        in_specs=[in_hbm],
-        out_specs=[in_hbm] * 2,
+        out_shape=[pltpu.HBM(bundle_shape.shape, BF16)] * 2
+        + [jax.ShapeDtypeStruct((NEAR, *inverses.shape[1:]), BF16)],
+        in_specs=[in_hbm] * 2,
+        out_specs=[in_hbm] * 2 + [IN_VMEM],
         scratch_shapes=[
             pltpu.VMEM(coupling.shape, BF16),
             pltpu.VMEM(bundle_shape.shape, BF16),
             pltpu.VMEM(bundle_shape.shape, BF16),
             pltpu.SemaphoreType.DMA((3, SEGMENT)),
+            pltpu.SemaphoreType.DMA,
         ],
         compiler_params=params(32),
         cost_estimate=pl.CostEstimate(flops=0, bytes_accessed=4 * coupling.size, transcendentals=0),
         name="bundle",
-    )(hbm(coupling))
-    *forcings, even, odd, bundle_a, end_a = pl.pallas_call(
+    )(hbm(coupling), hbm(inverses))
+    *forcings, bundle_a, end_a = pl.pallas_call(
         forcing_kernel,
-        out_shape=[forcing_shape] * 2 + [hot_shape] * 2 + [bundle_shape, state_shape],
-        in_specs=[IN_VMEM] * 3 + [in_hbm] * 2,
-        out_specs=[IN_VMEM] * 6,
+        out_shape=[forcing_shape] * 2 + [bundle_shape, state_shape],
+        in_specs=[IN_VMEM] * 4 + [in_hbm] * 2,
+        out_specs=[IN_VMEM] * 4,
         scratch_shapes=[
             pltpu.VMEM(packed_rows, F32),
             pltpu.VMEM((SEGMENT, FEATURES, LINES), F32),
@@ -394,8 +421,7 @@
         ],
         compiler_params=params(24),
         name="forcing",
-    )(arrived, cells, slot_counts, hbm(inverses), hbm(bundles[0]))
-    even, odd = vmem(even), vmem(odd)
+    )(arrived, cells, slot_counts, vmem(near), hbm(inverses), hbm(bundles[0]))
     forcings = [vmem(forcing) for forcing in forcings]
     end_b, bundle_b = pl.pallas_call(
         first_hop_kernel,
@@ -441,6 +467,15 @@
             name=name + "ab"[side],
         )(*operands)
 
+    cells, counts, _ = lax.optimization_barrier((cells, slot_counts, end_b))
+    even, odd = pl.pallas_call(
+        hots_kernel,
+        out_shape=[hot_shape] * 2,
+        in_specs=[IN_VMEM] * 2,
+        out_specs=[IN_VMEM] * 2,
+        compiler_params=params(8),
+        name="hots",
+    )(cells, counts)
     arrivals = ([], [])
     for hop in range(2 * N_CIRC - 1):
         for side in range(2):
@@ -462,7 +497,7 @@
         out_specs=IN_VMEM,
         compiler_params=params(16),
         name="return_pack",
-    )(*solved, even, odd)
+    )(*solved, vmem(even), vmem(odd))
     returned = exchange(returning)
     return pl.pallas_call(
         return_kernel,

time: 139 us -> 137 us (0.986)
  Pallas kernels: 30.9 us -> 29.1 us
    pallas_call x1 -> x2, Pallas kernels: 7.45 us -> 5.11 us  [the longest x1 4.58 us: local(): pl.pallas_call(forcing_kernel, out_shape=[forcing_shape] * 2 + [bundle_sh...]
  transfers between devices with their start and end apart: 31 -> 31, of which waited for: 4 -> 4; matrix products, arithmetic and copies ran while one was open for 0% -> 0% of each run, Pallas kernels for 12% -> 13%
where the time goes in v5:
time: 137 us; the launch traced here: 136 us
  blocking collectives  49.2 us (36%)
  starting transfers between devices  35.5 us (26%)
  Pallas kernels  29.1 us (21%)
  waiting for transfers between devices  20.6 us (15%)
    all_to_all x1, blocking collectives, exchange(): lax.all_to_all(blocks, ('circ', 'span'), split_axis=0, concat_axis=0, til...  49.2 us
    ppermute x30, starting transfers between devices, local(): arrivals[side].append(lax.ppermute(end, 'circ', [pair]))  24 us
    ppermute x30, waiting for transfers between devices, local(): arrivals[side].append(lax.ppermute(end, 'circ', [pair]))  18.2 us
    all_to_all x1, starting transfers between devices, exchange(): lax.all_to_all(blocks, ('circ', 'span'), split_axis=0, concat_axis=0, til...  11.5 us
    pallas_call x1, Pallas kernels, local(): pl.pallas_call(bundle_kernel, out_shape=[pltpu.HBM(bundle_shape.shape, BF...  8.38 us
    pallas_call x1, Pallas kernels, local(): pl.pallas_call(forcing_kernel, out_shape=[forcing_shape] * 2 + [bundle_sh...  4.58 us
    pallas_call x30, Pallas kernels, sweep(): pl.pallas_call(kernel, out_shape=shape, in_specs=[IN_VMEM] * len(operands...  4.17 us
  transfers between devices with their start and end apart: 31, of which 4 were waited for; matrix products, arithmetic and copies ran while one was open for 0% of the time, Pallas kernels for 13%

profile of v5, /device:TPU:1, one launch (start us, length us, event | category | flops | bytes accessed | tf_op | source)
XLA Modules:
  0.0 135.8 jit_solution(8120995194219872741)
XLA Ops:
  0.0 0.7 copy-done.1
  0.7 2.5 %pack_rows.1 = bf16[1024,128]{1,0:T(8,128)(2,1)} custom-call(bf16[80,768]{1,0:T(8,128)(2,1)} %rows_hbm.1, s32[12,1,128]{2,1,0:T(1,128)S(1)} %bitcast.11), custom_call_target="tpu_custom_call" | custom-call | tf_op jit(solution)/shard_map/pack_rows/pallas_call | solution.py:379
  3.2 11.5 %all-to-all-start = ((bf16[128,8,128]{2,1,0:T(8,128)(2,1)}), bf16[128,8,128]{2,1,0:T(8,128)(2,1)S(1)}, u32[]{:S(2)}, u32[]{:S(2)}) async-start(bf16[128,8,128]{2,1,0:T(8,128)(2,1)} %bitcast.1), calls=%async_computation | async-start | bytes 524288 | tf_op jit(solution)/shard_map/all_to_all | solution.py:366
  14.7 8.4 %bundle.1 = (bf16[6,40,80,128]{3,2,1,0:T(8,128)(2,1)}, bf16[6,40,80,128]{3,2,1,0:T(8,128)(2,1)}, bf16[2,80,80,128]{3,2,1,0:T(8,128)(2,1)S(1)}) custom-call(bf16[6,80,80,128]{3,2,1,0:T(8,128)(2,1)} %coupling_hbm.1, bf16[6,80,80,128]{3,2,1,0:T(8,128)(2,1)} %inverses_hbm.3), custom_call_target="tpu_custom_call" | custom-call | bytes 19660800 | tf_op jit(solution)/shard_map/bundle/pallas_call | solution.py:393
  23.1 2.4 %all-to-all-done = bf16[128,8,128]{2,1,0:T(8,128)(2,1)S(1)} async-done(((bf16[128,8,128]{2,1,0:T(8,128)(2,1)}), bf16[128,8,128]{2,1,0:T(8,128)(2,1)S(1)}, u32[]{:S(2)}, u32[]{:S(2)}) %all-to-all-start) | async-done | bytes 262176 | tf_op jit(solution)/shard_map/all_to_all | solution.py:366
  25.6 4.6 %forcing.1 = (f32[6,40,128]{2,1,0:T(8,128)S(1)}, f32[6,40,128]{2,1,0:T(8,128)S(1)}, bf16[6,40,80,128]{3,2,1,0:T(8,128)(2,1)S(1)}, f32[40,128]{1,0:T(8,128)S(1)}) custom-call(bf16[1024,128]{1,0:T(8,128)(2,1)S(1)} %bitcast.8, s32[12,1,128]{2,1,0:T(1,128)S(1)} %bitcast.9, s32[1,128]{1,0:T(1,128)S(1)} %copy-done.3, ...), custom_call_target="tpu_custom_call" | custom-call | tf_op jit(solution)/shard_map/forcing/pallas_call | solution.py:410
  30.2 1.6 %collective-permute-start = (f32[40,128]{1,0:T(8,128)S(1)}, f32[40,128]{1,0:T(8,128)S(1)}, u32[]{:S(2)}, u32[]{:S(2)}) collective-permute-start(f32[40,128]{1,0:T(8,128)S(1)} %get-tuple-element.20), channel_id=1, source_target_pairs={{0,16},{1,17},{2,18},{3,19},{4,20},{5,21},{6,22},{7,23},{8,24},{9,... | collective-permute-start | bytes 61448 | tf_op jit(solution)/shard_map/ppermute | solution.py:487
  31.8 2.4 %first_hop.1 = (f32[40,128]{1,0:T(8,128)S(1)}, bf16[6,40,80,128]{3,2,1,0:T(8,128)(2,1)S(1)}) custom-call(bf16[6,40,80,128]{3,2,1,0:T(8,128)(2,1)} %get-tuple-element.23.bundle_hbm, f32[6,40,128]{2,1,0:T(8,128)S(1)} %get-tuple-element.24.forcing_ref.refs_9_), custom_call_target="tpu_custom_call" | custom-call | tf_op jit(solution)/shard_map/first_hop/pallas_call | solution.py:426
  34.2 1.3 collective-permute-start.15
  35.5 1.3 widen.2.coupling_ref.refs_8_
  36.8 1.3 widen.3.coupling_ref.refs_8_
  38.1 0.7 collective-permute-start.1
  38.8 0.7 collective-permute-start.16
  39.5 0.7 collective-permute-start.2
  40.2 0.7 collective-permute-start.17
  40.9 0.7 collective-permute-start.3
  41.6 0.7 collective-permute-start.18
  42.3 0.7 collective-permute-start.4
  43.2 0.7 collective-permute-start.19
  43.9 0.7 collective-permute-start.5
  44.6 0.7 collective-permute-start.20
  45.3 0.7 collective-permute-start.6
  46.0 0.7 collective-permute-start.21
  46.7 1.3 collective-permute-start.7
  48.1 1.3 collective-permute-start.22
  49.4 17.6 %collective-permute-done.7.state_ref.refs_0_ = f32[40,128]{1,0:T(8,128)S(1)} collective-permute-done((f32[40,128]{1,0:T(8,128)S(1)}, f32[40,128]{1,0:T(8,128)S(1)}, u32[]{:S(2)}, u32[]{:S(2)}) %collective-permute-start.7) | collective-permute-done | bytes 20512 | tf_op jit(solution)/shard_map/ppermute | solution.py:487
  66.9 0.8 hop_a.21
  67.8 1.3 collective-permute-start.8
  69.4 0.8 hop_b.21
  70.2 1.3 collective-permute-start.23
  71.6 0.7 collective-permute-start.9
  72.4 0.7 collective-permute-start.24
  73.1 0.7 collective-permute-start.10
  73.8 0.7 collective-permute-start.25
  74.8 0.7 collective-permute-start.11
  75.5 0.7 collective-permute-start.26
  76.2 0.7 collective-permute-start.12
  76.9 0.7 collective-permute-start.27
  77.6 0.7 collective-permute-start.13
  78.3 0.7 collective-permute-start.28
  79.0 0.7 collective-permute-start.14
  79.7 0.7 collective-permute-start.29
  80.4 0.5 hots.1
  80.9 0.8 final_a.1.solved_a
  81.8 0.8 final_b.1.solved_b
  82.6 1.5 %return_pack.1 = f32[1024,128]{1,0:T(8,128)S(1)} custom-call(f32[6,40,128]{2,1,0:T(8,128)S(1)} %final_a.1.solved_a, f32[6,40,128]{2,1,0:T(8,128)S(1)} %final_b.1.solved_b, bf16[768,768]{1,0:T(8,128)(2,1)S(1)} %get-tuple-element.29.even_ref, bf16[768,768]{1,0:T(8,128)(2,1)S(1)} %get-tuple-element.30.odd_ref), custom_call_target="tpu_custom_call" | custom-call | tf_op jit(solution)/shard_map/return_pack/pallas_call | solution.py:493
  84.2 49.2 %all_to_all.10 = f32[128,8,128]{2,1,0:T(8,128)S(1)} all-to-all(f32[128,8,128]{2,1,0:T(8,128)S(1)} %bitcast.7), channel_id=1, replica_groups=mesh['circ'=8,'span'=16] {'circ','span'}, dimensions={0} | all-to-all | bytes 1048576 | tf_op jit(solution)/shard_map/all_to_all | solution.py:366
  133.4 2.5 %return_rows.1 = f32[80,768]{1,0:T(8,128)} custom-call(f32[1024,128]{1,0:T(8,128)S(1)} %bitcast.6, s32[12,1,128]{2,1,0:T(1,128)S(1)} %bitcast.12), custom_call_target="tpu_custom_call" | custom-call | tf_op jit(solution)/shard_map/return_rows/pallas_call | solution.py:502
  (62 shorter events, 1.4 us)
Async XLA Ops:
  0.0 0.7 copy-start.1
  3.2 22.4 %all-to-all-start = ((bf16[128,8,128]{2,1,0:T(8,128)(2,1)}), bf16[128,8,128]{2,1,0:T(8,128)(2,1)S(1)}, u32[]{:S(2)}, u32[]{:S(2)}) async-start(bf16[128,8,128]{2,1,0:T(8,128)(2,1)} %bitcast.1), calls=%async_computation | async-start | bytes 524288 | tf_op jit(solution)/shard_map/all_to_all | solution.py:366
  14.7 10.9 %copy-start = (s32[1,128,12]{1,0,2:T(1,128)S(1)}, s32[1,128,12]{1,0,2:T(1,128)}, u32[]{:S(2)}) copy-start(s32[1,128,12]{1,0,2:T(1,128)} %param.10) | copy-start | bytes 18436
  14.7 10.8 %copy-start.3 = (s32[1,128]{1,0:T(1,128)S(1)}, s32[1,128]{1,0:T(1,128)}, u32[]{:S(2)}) copy-start(s32[1,128]{1,0:T(1,128)} %counts_ref.2) | copy-start | bytes 1540
  30.2 7.9 %collective-permute-start = (f32[40,128]{1,0:T(8,128)S(1)}, f32[40,128]{1,0:T(8,128)S(1)}, u32[]{:S(2)}, u32[]{:S(2)}) collective-permute-start(f32[40,128]{1,0:T(8,128)S(1)} %get-tuple-element.20), channel_id=1, source_target_pairs={{0,16},{1,17},{2,18},{3,19},{4,20},{5,21},{6,22},{7,23},{8,24},{9,... | collective-permute-start | bytes 61448 | tf_op jit(solution)/shard_map/ppermute | solution.py:487
  34.2 4.6 %collective-permute-start.15 = (f32[40,128]{1,0:T(8,128)S(1)}, f32[40,128]{1,0:T(8,128)S(1)}, u32[]{:S(2)}, u32[]{:S(2)}) collective-permute-start(f32[40,128]{1,0:T(8,128)S(1)} %get-tuple-element.25), channel_id=1, source_target_pairs={{0,16},{1,17},{2,18},{3,19},{4,20},{5,21},{6,22},{7,23},{8,24},{9,... | collective-permute-start | bytes 61448 | tf_op jit(solution)/shard_map/ppermute | solution.py:487
  38.1 1.4 %collective-permute-start.1 = (f32[40,128]{1,0:T(8,128)S(1)}, f32[40,128]{1,0:T(8,128)S(1)}, u32[]{:S(2)}, u32[]{:S(2)}) collective-permute-start(f32[40,128]{1,0:T(8,128)S(1)} %hop_a.14), channel_id=1, source_target_pairs={{16,32},{17,33},{18,34},{19,35},{20,36},{21,37},{22,38},{23,39},{2... | collective-permute-start | bytes 61448 | tf_op jit(solution)/shard_map/ppermute | solution.py:487
  38.8 1.4 %collective-permute-start.16 = (f32[40,128]{1,0:T(8,128)S(1)}, f32[40,128]{1,0:T(8,128)S(1)}, u32[]{:S(2)}, u32[]{:S(2)}) collective-permute-start(f32[40,128]{1,0:T(8,128)S(1)} %hop_b.14), channel_id=1, source_target_pairs={{16,32},{17,33},{18,34},{19,35},{20,36},{21,37},{22,38},{23,39},{2... | collective-permute-start | bytes 61448 | tf_op jit(solution)/shard_map/ppermute | solution.py:487
  39.5 1.4 %collective-permute-start.2 = (f32[40,128]{1,0:T(8,128)S(1)}, f32[40,128]{1,0:T(8,128)S(1)}, u32[]{:S(2)}, u32[]{:S(2)}) collective-permute-start(f32[40,128]{1,0:T(8,128)S(1)} %hop_a.15), channel_id=1, source_target_pairs={{32,48},{33,49},{34,50},{35,51},{36,52},{37,53},{38,54},{39,55},{4... | collective-permute-start | bytes 61448 | tf_op jit(solution)/shard_map/ppermute | solution.py:487
  40.2 1.4 %collective-permute-start.17 = (f32[40,128]{1,0:T(8,128)S(1)}, f32[40,128]{1,0:T(8,128)S(1)}, u32[]{:S(2)}, u32[]{:S(2)}) collective-permute-start(f32[40,128]{1,0:T(8,128)S(1)} %hop_b.15), channel_id=1, source_target_pairs={{32,48},{33,49},{34,50},{35,51},{36,52},{37,53},{38,54},{39,55},{4... | collective-permute-start | bytes 61448 | tf_op jit(solution)/shard_map/ppermute | solution.py:487
  40.9 1.4 %collective-permute-start.3 = (f32[40,128]{1,0:T(8,128)S(1)}, f32[40,128]{1,0:T(8,128)S(1)}, u32[]{:S(2)}, u32[]{:S(2)}) collective-permute-start(f32[40,128]{1,0:T(8,128)S(1)} %hop_a.16), channel_id=1, source_target_pairs={{48,64},{49,65},{50,66},{51,67},{52,68},{53,69},{54,70},{55,71},{5... | collective-permute-start | bytes 61448 | tf_op jit(solution)/shard_map/ppermute | solution.py:487
  41.6 1.4 %collective-permute-start.18 = (f32[40,128]{1,0:T(8,128)S(1)}, f32[40,128]{1,0:T(8,128)S(1)}, u32[]{:S(2)}, u32[]{:S(2)}) collective-permute-start(f32[40,128]{1,0:T(8,128)S(1)} %hop_b.16), channel_id=1, source_target_pairs={{48,64},{49,65},{50,66},{51,67},{52,68},{53,69},{54,70},{55,71},{5... | collective-permute-start | bytes 61448 | tf_op jit(solution)/shard_map/ppermute | solution.py:487
  42.3 1.6 %collective-permute-start.4 = (f32[40,128]{1,0:T(8,128)S(1)}, f32[40,128]{1,0:T(8,128)S(1)}, u32[]{:S(2)}, u32[]{:S(2)}) collective-permute-start(f32[40,128]{1,0:T(8,128)S(1)} %hop_a.17), channel_id=1, source_target_pairs={{64,80},{65,81},{66,82},{67,83},{68,84},{69,85},{70,86},{71,87},{7... | collective-permute-start | bytes 61448 | tf_op jit(solution)/shard_map/ppermute | solution.py:487
  43.2 1.4 %collective-permute-start.19 = (f32[40,128]{1,0:T(8,128)S(1)}, f32[40,128]{1,0:T(8,128)S(1)}, u32[]{:S(2)}, u32[]{:S(2)}) collective-permute-start(f32[40,128]{1,0:T(8,128)S(1)} %hop_b.17), channel_id=1, source_target_pairs={{64,80},{65,81},{66,82},{67,83},{68,84},{69,85},{70,86},{71,87},{7... | collective-permute-start | bytes 61448 | tf_op jit(solution)/shard_map/ppermute | solution.py:487
  43.9 1.4 %collective-permute-start.5 = (f32[40,128]{1,0:T(8,128)S(1)}, f32[40,128]{1,0:T(8,128)S(1)}, u32[]{:S(2)}, u32[]{:S(2)}) collective-permute-start(f32[40,128]{1,0:T(8,128)S(1)} %hop_a.18), channel_id=1, source_target_pairs={{80,96},{81,97},{82,98},{83,99},{84,100},{85,101},{86,102},{87,103... | collective-permute-start | bytes 61448 | tf_op jit(solution)/shard_map/ppermute | solution.py:487
  44.6 1.4 %collective-permute-start.20 = (f32[40,128]{1,0:T(8,128)S(1)}, f32[40,128]{1,0:T(8,128)S(1)}, u32[]{:S(2)}, u32[]{:S(2)}) collective-permute-start(f32[40,128]{1,0:T(8,128)S(1)} %hop_b.18), channel_id=1, source_target_pairs={{80,96},{81,97},{82,98},{83,99},{84,100},{85,101},{86,102},{87,103... | collective-permute-start | bytes 61448 | tf_op jit(solution)/shard_map/ppermute | solution.py:487
  45.3 1.4 %collective-permute-start.6 = (f32[40,128]{1,0:T(8,128)S(1)}, f32[40,128]{1,0:T(8,128)S(1)}, u32[]{:S(2)}, u32[]{:S(2)}) collective-permute-start(f32[40,128]{1,0:T(8,128)S(1)} %hop_a.19), channel_id=1, source_target_pairs={{96,112},{97,113},{98,114},{99,115},{100,116},{101,117},{102,118},... | collective-permute-start | bytes 61448 | tf_op jit(solution)/shard_map/ppermute | solution.py:487
  46.0 2.0 %collective-permute-start.21 = (f32[40,128]{1,0:T(8,128)S(1)}, f32[40,128]{1,0:T(8,128)S(1)}, u32[]{:S(2)}, u32[]{:S(2)}) collective-permute-start(f32[40,128]{1,0:T(8,128)S(1)} %hop_b.19), channel_id=1, source_target_pairs={{96,112},{97,113},{98,114},{99,115},{100,116},{101,117},{102,118},... | collective-permute-start | bytes 61448 | tf_op jit(solution)/shard_map/ppermute | solution.py:487
  46.7 20.2 %collective-permute-start.7 = (f32[40,128]{1,0:T(8,128)S(1)}, f32[40,128]{1,0:T(8,128)S(1)}, u32[]{:S(2)}, u32[]{:S(2)}) collective-permute-start(f32[40,128]{1,0:T(8,128)S(1)} %hop_a.20), channel_id=1, source_target_pairs={{112,0},{113,1},{114,2},{115,3},{116,4},{117,5},{118,6},{119,7},{1... | collective-permute-start | bytes 61448 | tf_op jit(solution)/shard_map/ppermute | solution.py:487
  48.1 21.3 %collective-permute-start.22 = (f32[40,128]{1,0:T(8,128)S(1)}, f32[40,128]{1,0:T(8,128)S(1)}, u32[]{:S(2)}, u32[]{:S(2)}) collective-permute-start(f32[40,128]{1,0:T(8,128)S(1)} %hop_b.20), channel_id=1, source_target_pairs={{112,0},{113,1},{114,2},{115,3},{116,4},{117,5},{118,6},{119,7},{1... | collective-permute-start | bytes 61448 | tf_op jit(solution)/shard_map/ppermute | solution.py:487
  67.8 3.8 %collective-permute-start.8 = (f32[40,128]{1,0:T(8,128)S(1)}, f32[40,128]{1,0:T(8,128)S(1)}, u32[]{:S(2)}, u32[]{:S(2)}) collective-permute-start(f32[40,128]{1,0:T(8,128)S(1)} %hop_a.21), channel_id=1, source_target_pairs={{0,16},{1,17},{2,18},{3,19},{4,20},{5,21},{6,22},{7,23},{8,24},{9,... | collective-permute-start | bytes 61448 | tf_op jit(solution)/shard_map/ppermute | solution.py:487
  70.2 2.2 %collective-permute-start.23 = (f32[40,128]{1,0:T(8,128)S(1)}, f32[40,128]{1,0:T(8,128)S(1)}, u32[]{:S(2)}, u32[]{:S(2)}) collective-permute-start(f32[40,128]{1,0:T(8,128)S(1)} %hop_b.21), channel_id=1, source_target_pairs={{0,16},{1,17},{2,18},{3,19},{4,20},{5,21},{6,22},{7,23},{8,24},{9,... | collective-permute-start | bytes 61448 | tf_op jit(solution)/shard_map/ppermute | solution.py:487
  71.6 1.5 %collective-permute-start.9 = (f32[40,128]{1,0:T(8,128)S(1)}, f32[40,128]{1,0:T(8,128)S(1)}, u32[]{:S(2)}, u32[]{:S(2)}) collective-permute-start(f32[40,128]{1,0:T(8,128)S(1)} %hop_a.22), channel_id=1, source_target_pairs={{16,32},{17,33},{18,34},{19,35},{20,36},{21,37},{22,38},{23,39},{2... | collective-permute-start | bytes 61448 | tf_op jit(solution)/shard_map/ppermute | solution.py:487
  72.4 1.4 %collective-permute-start.24 = (f32[40,128]{1,0:T(8,128)S(1)}, f32[40,128]{1,0:T(8,128)S(1)}, u32[]{:S(2)}, u32[]{:S(2)}) collective-permute-start(f32[40,128]{1,0:T(8,128)S(1)} %hop_b.22), channel_id=1, source_target_pairs={{16,32},{17,33},{18,34},{19,35},{20,36},{21,37},{22,38},{23,39},{2... | collective-permute-start | bytes 61448 | tf_op jit(solution)/shard_map/ppermute | solution.py:487
  73.1 1.4 %collective-permute-start.10 = (f32[40,128]{1,0:T(8,128)S(1)}, f32[40,128]{1,0:T(8,128)S(1)}, u32[]{:S(2)}, u32[]{:S(2)}) collective-permute-start(f32[40,128]{1,0:T(8,128)S(1)} %hop_a.23), channel_id=1, source_target_pairs={{32,48},{33,49},{34,50},{35,51},{36,52},{37,53},{38,54},{39,55},{4... | collective-permute-start | bytes 61448 | tf_op jit(solution)/shard_map/ppermute | solution.py:487
  73.8 1.6 %collective-permute-start.25 = (f32[40,128]{1,0:T(8,128)S(1)}, f32[40,128]{1,0:T(8,128)S(1)}, u32[]{:S(2)}, u32[]{:S(2)}) collective-permute-start(f32[40,128]{1,0:T(8,128)S(1)} %hop_b.23), channel_id=1, source_target_pairs={{32,48},{33,49},{34,50},{35,51},{36,52},{37,53},{38,54},{39,55},{4... | collective-permute-start | bytes 61448 | tf_op jit(solution)/shard_map/ppermute | solution.py:487
  74.8 1.4 %collective-permute-start.11 = (f32[40,128]{1,0:T(8,128)S(1)}, f32[40,128]{1,0:T(8,128)S(1)}, u32[]{:S(2)}, u32[]{:S(2)}) collective-permute-start(f32[40,128]{1,0:T(8,128)S(1)} %hop_a.24), channel_id=1, source_target_pairs={{48,64},{49,65},{50,66},{51,67},{52,68},{53,69},{54,70},{55,71},{5... | collective-permute-start | bytes 61448 | tf_op jit(solution)/shard_map/ppermute | solution.py:487
  75.5 1.4 %collective-permute-start.26 = (f32[40,128]{1,0:T(8,128)S(1)}, f32[40,128]{1,0:T(8,128)S(1)}, u32[]{:S(2)}, u32[]{:S(2)}) collective-permute-start(f32[40,128]{1,0:T(8,128)S(1)} %hop_b.24), channel_id=1, source_target_pairs={{48,64},{49,65},{50,66},{51,67},{52,68},{53,69},{54,70},{55,71},{5... | collective-permute-start | bytes 61448 | tf_op jit(solution)/shard_map/ppermute | solution.py:487
  76.2 1.4 %collective-permute-start.12 = (f32[40,128]{1,0:T(8,128)S(1)}, f32[40,128]{1,0:T(8,128)S(1)}, u32[]{:S(2)}, u32[]{:S(2)}) collective-permute-start(f32[40,128]{1,0:T(8,128)S(1)} %hop_a.25), channel_id=1, source_target_pairs={{64,80},{65,81},{66,82},{67,83},{68,84},{69,85},{70,86},{71,87},{7... | collective-permute-start | bytes 61448 | tf_op jit(solution)/shard_map/ppermute | solution.py:487
  76.9 1.4 %collective-permute-start.27 = (f32[40,128]{1,0:T(8,128)S(1)}, f32[40,128]{1,0:T(8,128)S(1)}, u32[]{:S(2)}, u32[]{:S(2)}) collective-permute-start(f32[40,128]{1,0:T(8,128)S(1)} %hop_b.25), channel_id=1, source_target_pairs={{64,80},{65,81},{66,82},{67,83},{68,84},{69,85},{70,86},{71,87},{7... | collective-permute-start | bytes 61448 | tf_op jit(solution)/shard_map/ppermute | solution.py:487
  77.6 1.4 %collective-permute-start.13 = (f32[40,128]{1,0:T(8,128)S(1)}, f32[40,128]{1,0:T(8,128)S(1)}, u32[]{:S(2)}, u32[]{:S(2)}) collective-permute-start(f32[40,128]{1,0:T(8,128)S(1)} %hop_a.26), channel_id=1, source_target_pairs={{80,96},{81,97},{82,98},{83,99},{84,100},{85,101},{86,102},{87,103... | collective-permute-start | bytes 61448 | tf_op jit(solution)/shard_map/ppermute | solution.py:487
  78.3 1.4 %collective-permute-start.28 = (f32[40,128]{1,0:T(8,128)S(1)}, f32[40,128]{1,0:T(8,128)S(1)}, u32[]{:S(2)}, u32[]{:S(2)}) collective-permute-start(f32[40,128]{1,0:T(8,128)S(1)} %hop_b.26), channel_id=1, source_target_pairs={{80,96},{81,97},{82,98},{83,99},{84,100},{85,101},{86,102},{87,103... | collective-permute-start | bytes 61448 | tf_op jit(solution)/shard_map/ppermute | solution.py:487
  79.0 1.9 %collective-permute-start.14 = (f32[40,128]{1,0:T(8,128)S(1)}, f32[40,128]{1,0:T(8,128)S(1)}, u32[]{:S(2)}, u32[]{:S(2)}) collective-permute-start(f32[40,128]{1,0:T(8,128)S(1)} %hop_a.27), channel_id=1, source_target_pairs={{96,112},{97,113},{98,114},{99,115},{100,116},{101,117},{102,118},... | collective-permute-start | bytes 61448 | tf_op jit(solution)/shard_map/ppermute | solution.py:487
  79.7 2.1 %collective-permute-start.29 = (f32[40,128]{1,0:T(8,128)S(1)}, f32[40,128]{1,0:T(8,128)S(1)}, u32[]{:S(2)}, u32[]{:S(2)}) collective-permute-start(f32[40,128]{1,0:T(8,128)S(1)} %hop_b.27), channel_id=1, source_target_pairs={{96,112},{97,113},{98,114},{99,115},{100,116},{101,117},{102,118},... | collective-permute-start | bytes 61448 | tf_op jit(solution)/shard_map/ppermute | solution.py:487
  81.8 51.6 %copy-start.2 = (s32[1,128,12]{1,0,2:T(1,128)S(1)}, s32[1,128,12]{1,0,2:T(1,128)}, u32[]{:S(2)}) copy-start(s32[1,128,12]{1,0,2:T(1,128)} %param.9) | copy-start | bytes 18436
